TPU v7x, 32 devices: a whole 2x2x4 slice. The times are simulated.
32 devices in a mesh: dp: 8 (over z, y), pipe: 4 (over x, core).
Axes of the slice: x: 2, y: 2, z: 4, core: 2. Of those that a mesh axis runs over, the one named last changes fastest.
Arguments:
- tokens: bfloat16 [32, 512, 768], P('dp'), may hold values from -18 to 18
- lengths: int32 [32], P('dp'), may hold values from 8 to 512, as said below
- ema_scales: float32 [4, 4], P('pipe'), may hold values from 2 to 6
- w_qkv: bfloat16 [4, 768, 2304], P('pipe'), may hold values from -0.21875 to 0.21875
- bias_qv: float32 [4, 1536], P('pipe'), may hold values from -4 to 4
- w_out: bfloat16 [4, 768, 768], P('pipe'), may hold values from -0.875 to 0.875
- bias_out: float32 [4, 768], P('pipe'), may hold values from -4 to 4
- w_up: bfloat16 [4, 768, 3072], P('pipe'), may hold values from -0.21875 to 0.21875
- bias_up: float32 [4, 3072], P('pipe'), may hold values from -4 to 4
- w_down: bfloat16 [4, 3072, 768], P('pipe'), may hold values from -0.109375 to 0.109375
- bias_down: float32 [4, 768], P('pipe'), may hold values from -4 to 4
- ln_gain: float32 [4, 2, 768], P('pipe'), may hold values from 0.5 to 1.5
- ln_bias: float32 [4, 2, 768], P('pipe'), may hold values from -4 to 4
- cotangent: bfloat16 [32, 512, 768], P('dp'), may hold values from -6 to 6
Outputs:
- mixed: bfloat16 [32, 512, 768], P('dp', 'pipe')
- grad_tokens: bfloat16 [32, 512, 768], P('dp', 'pipe')
- grad_w_qkv: float32 [4, 768, 2304], P('pipe', 'dp')
- grad_bias_qv: float32 [4, 1536], P('pipe', 'dp')
- grad_w_out: float32 [4, 768, 768], P('pipe', 'dp')
- grad_bias_out: float32 [4, 768], P('pipe', 'dp')
- grad_w_up: float32 [4, 768, 3072], P('pipe', 'dp')
- grad_bias_up: float32 [4, 3072], P('pipe', 'dp')
- grad_w_down: float32 [4, 3072, 768], P('pipe', 'dp')
- grad_bias_down: float32 [4, 768], P('pipe', 'dp')
- grad_ln_gain: float32 [4, 2, 768], P('pipe', None, 'dp')
- grad_ln_bias: float32 [4, 2, 768], P('pipe', None, 'dp')
- batch_max: float32 [4, 4], P('pipe')
Inputs may be any that keep to these rules, and one draw needn't show every extreme that they name: `lengths`: each row holds one sequence from position 0: either of 8 to 128 tokens or of more than 128; the rest of its 512 positions is padding. Some row holds 512 tokens.
All inputs are finite; a program needn't handle non-finite values.
Results may differ from a plain program's by a relative error of at most 0.02.
The roundings to bfloat16 on the way count: a program that leaves them out, or rounds other values in their place, can miss the bound.
Values may be sent and summed in bfloat16 or wider, within the bound.
A program may use at most 576 MiB of HBM per device.

v0:
```python
from functools import partial

import jax
import jax.numpy as jnp
from jax import lax
from jax.sharding import PartitionSpec as P

HEAD_DIM = 64
MICRO = 4


norm_eps = 1e-06
mask_fill = -1000000000.0


def from_behind(x, axis, by):
    devices = lax.axis_size(axis)
    pairs = [(i, i + by) for i in range(devices) if 0 <= i + by < devices]
    return lax.ppermute(x, axis, pairs)


def squash(signal, ceiling):
    return ceiling * jnp.tanh(signal / ceiling)


def squash_slope(signal, ceiling):
    tanh_ratio = jnp.tanh(signal / ceiling)
    return 1.0 - tanh_ratio * tanh_ratio


def layer_norm(signal, gain_vec, shift_vec):
    center = signal - jnp.mean(signal, -1, keepdims=True)
    spread = jnp.mean(center * center, -1, keepdims=True)
    return center * lax.rsqrt(spread + norm_eps) * gain_vec + shift_vec


def matmul(left_op, right_op):
    return jnp.einsum("rsd,de->rse", left_op, right_op, preferred_element_type=jnp.float32)


def matmul_back(left_op, right_op):
    return jnp.einsum("rse,de->rsd", left_op, right_op, preferred_element_type=jnp.float32)


def weight_grad(left_op, right_op):
    return jnp.einsum("rsd,rse->de", left_op, right_op, preferred_element_type=jnp.float32)


def column_sum(signal):
    return jnp.sum(signal.astype(jnp.float32), (0, 1))


def split_heads(signal):
    return signal.reshape(signal.shape[0], signal.shape[1] // HEAD_DIM, HEAD_DIM)


def row_scores(queries, keys_low, length):
    seq_len = queries.shape[0]
    scores = jnp.einsum(
        "qhd,khd->hqk",
        split_heads(queries),
        split_heads(keys_low),
        preferred_element_type=jnp.float32,
    ) * HEAD_DIM ** (-0.5)
    key_mask = jnp.arange(seq_len) < length
    return jnp.where(key_mask[None, None, :], scores, mask_fill)


def attend_row(operands):
    queries, keys_low, values_low, length = operands
    scores = row_scores(queries, keys_low, length)
    row_top = jnp.max(scores, -1, keepdims=True)
    weights = jnp.exp(scores - row_top)
    row_total = jnp.sum(weights, -1, keepdims=True)
    probabilities = (weights / row_total).astype(jnp.bfloat16)
    context = jnp.einsum(
        "hqk,khd->qhd", probabilities, split_heads(values_low), preferred_element_type=jnp.float32
    )
    return (context.reshape(queries.shape), row_top + jnp.log(row_total))


def attend_back(operands):
    queries, keys_low, values_low, length, log_total, grad_context = operands
    score_scale = HEAD_DIM ** (-0.5)
    probabilities = jnp.exp(row_scores(queries, keys_low, length) - log_total)
    grad_heads = split_heads(grad_context)
    grad_values = jnp.einsum(
        "hqk,qhd->khd",
        probabilities.astype(jnp.bfloat16),
        grad_heads,
        preferred_element_type=jnp.float32,
    )
    grad_probs = jnp.einsum(
        "qhd,khd->hqk", grad_heads, split_heads(values_low), preferred_element_type=jnp.float32
    )
    row_inner = jnp.sum(grad_probs * probabilities, -1, keepdims=True)
    grad_scores = (probabilities * (grad_probs - row_inner)).astype(jnp.bfloat16)
    grad_queries = (
        jnp.einsum(
            "hqk,khd->qhd", grad_scores, split_heads(keys_low), preferred_element_type=jnp.float32
        )
        * score_scale
    )
    grad_keys = (
        jnp.einsum(
            "hqk,qhd->khd", grad_scores, split_heads(queries), preferred_element_type=jnp.float32
        )
        * score_scale
    )
    grad_parts = [grad_queries, grad_keys, grad_values]
    return jnp.concatenate(
        [grad_piece.reshape(queries.shape).astype(jnp.bfloat16) for grad_piece in grad_parts], -1
    )


def layer_forward(layer_in, row_lengths, weights, ceilings):
    w_qkv, bias_qv, w_out, bias_out, w_up, bias_up, w_down, bias_down, ln_gain, ln_bias = weights
    model_width = layer_in.shape[-1]
    layer_f32 = layer_in.astype(jnp.float32)
    x_low = squash(layer_f32, ceilings[0]).astype(jnp.bfloat16)
    projected = matmul(x_low, w_qkv)
    queries = (projected[..., :model_width] + bias_qv[:model_width]).astype(jnp.bfloat16)
    keys_low = projected[..., model_width : 2 * model_width].astype(jnp.bfloat16)
    values_low = (projected[..., 2 * model_width :] + bias_qv[model_width:]).astype(jnp.bfloat16)
    context, log_total = lax.map(attend_row, (queries, keys_low, values_low, row_lengths))
    ctx_low = squash(context, ceilings[1]).astype(jnp.bfloat16)
    mixed_in = layer_f32 + (matmul(ctx_low, w_out) + bias_out)
    hidden = layer_norm(mixed_in, ln_gain[0], ln_bias[0])
    hid_low = squash(hidden, ceilings[2]).astype(jnp.bfloat16)
    up_pre = matmul(hid_low, w_up) + bias_up
    active = jax.nn.gelu(up_pre, approximate=False)
    act_low = squash(active, ceilings[3]).astype(jnp.bfloat16)
    second_in = hidden + (matmul(act_low, w_down) + bias_down)
    layer_out = layer_norm(second_in, ln_gain[1], ln_bias[1]).astype(jnp.bfloat16)
    valid_mask = jnp.arange(layer_in.shape[1])[None, :] < row_lengths[:, None]

    def masked_peak(signal):
        return jnp.max(jnp.where(valid_mask[..., None], jnp.abs(signal), 0.0))

    maxima = jnp.stack(
        [masked_peak(layer_f32), masked_peak(context), masked_peak(hidden), masked_peak(active)]
    )
    kept_state = (
        layer_in,
        x_low,
        queries,
        keys_low,
        values_low,
        log_total,
        context,
        ctx_low,
        mixed_in,
        hid_low,
        up_pre,
        act_low,
        second_in,
    )
    return (layer_out, kept_state, maxima)


def layer_backward(kept_state, grad_out, row_lengths, weights, ceilings):
    (
        layer_in,
        x_low,
        queries,
        keys_low,
        values_low,
        log_total,
        context,
        ctx_low,
        mixed_in,
        hid_low,
        up_pre,
        act_low,
        second_in,
    ) = kept_state
    w_qkv, bias_qv, w_out, bias_out, w_up, bias_up, w_down, bias_down, ln_gain, ln_bias = weights
    model_width = layer_in.shape[-1]
    second_pull = jax.vjp(layer_norm, second_in, ln_gain[1], ln_bias[1])[1]
    grad_second, gain_second, shift_second = second_pull(grad_out.astype(jnp.float32))
    grad_down = grad_second.astype(jnp.bfloat16)
    active, gelu_pull = jax.vjp(partial(jax.nn.gelu, approximate=False), up_pre)
    grad_active = matmul_back(grad_down, w_down) * squash_slope(active, ceilings[3])
    grad_up = gelu_pull(grad_active)[0].astype(jnp.bfloat16)
    hidden, first_pull = jax.vjp(layer_norm, mixed_in, ln_gain[0], ln_bias[0])
    grad_hidden = grad_second + matmul_back(grad_up, w_up) * squash_slope(hidden, ceilings[2])
    grad_mixed, gain_first, shift_first = first_pull(grad_hidden)
    grad_branch = grad_mixed.astype(jnp.bfloat16)
    grad_context = (matmul_back(grad_branch, w_out) * squash_slope(context, ceilings[1])).astype(
        jnp.bfloat16
    )
    grad_proj = lax.map(
        attend_back, (queries, keys_low, values_low, row_lengths, log_total, grad_context)
    )
    layer_f32 = layer_in.astype(jnp.float32)
    grad_in = (
        grad_mixed + matmul_back(grad_proj, w_qkv) * squash_slope(layer_f32, ceilings[0])
    ).astype(jnp.bfloat16)
    grad_bias_qv = jnp.concatenate(
        [column_sum(grad_proj[..., :model_width]), column_sum(grad_proj[..., 2 * model_width :])]
    )
    tick_grads = (
        weight_grad(x_low, grad_proj),
        grad_bias_qv,
        weight_grad(ctx_low, grad_branch),
        column_sum(grad_branch),
        weight_grad(hid_low, grad_up),
        column_sum(grad_up),
        weight_grad(act_low, grad_down),
        column_sum(grad_down),
        jnp.stack([gain_first, gain_second]),
        jnp.stack([shift_first, shift_second]),
    )
    return (grad_in, tick_grads)


def store_slot(buffer, fresh_state, slot_index, active_tick):

    def place_one(whole_buf, new_piece):
        old_piece = lax.dynamic_index_in_dim(whole_buf, slot_index, 0, keepdims=False)
        return lax.dynamic_update_index_in_dim(
            whole_buf, jnp.where(active_tick, new_piece, old_piece), slot_index, 0
        )

    return jax.tree.map(place_one, buffer, fresh_state)


def store_rows(whole_buf, new_rows, start_row, active_tick):
    old_rows = lax.dynamic_slice_in_dim(whole_buf, start_row, new_rows.shape[0], 0)
    return lax.dynamic_update_slice_in_dim(
        whole_buf, jnp.where(active_tick, new_rows, old_rows), start_row, 0
    )


def shards(
    tokens,
    lengths,
    ema_scales,
    w_qkv,
    bias_qv,
    w_out,
    bias_out,
    w_up,
    bias_up,
    w_down,
    bias_down,
    ln_gain,
    ln_bias,
    cotangent,
):
    section_count = lax.axis_size("pipe")
    section_index = lax.axis_index("pipe")
    block_rows = tokens.shape[0] // MICRO
    seq_len = tokens.shape[1]
    tick_count = MICRO + section_count - 1
    weights = (
        w_qkv[0],
        bias_qv[0],
        w_out[0],
        bias_out[0],
        w_up[0],
        bias_up[0],
        w_down[0],
        bias_down[0],
        ln_gain[0],
        ln_bias[0],
    )
    ceilings = ema_scales[0]
    is_first = section_index == 0
    is_last = section_index == section_count - 1
    incoming = jnp.zeros((block_rows,) + tokens.shape[1:], jnp.bfloat16)
    outputs = jnp.zeros(tokens.shape, jnp.bfloat16)
    stash = None
    peak_vals = jnp.zeros((4,), jnp.float32)
    for moment in range(tick_count):
        micro_id = moment - section_index
        active_tick = (micro_id >= 0) & (micro_id < MICRO)
        slot_index = jnp.clip(micro_id, 0, MICRO - 1)
        first_row = min(moment, MICRO - 1) * block_rows
        layer_in = jnp.where(is_first, tokens[first_row : first_row + block_rows], incoming)
        row_lengths = lax.dynamic_slice_in_dim(lengths, slot_index * block_rows, block_rows)
        layer_out, kept_state, maxima = layer_forward(layer_in, row_lengths, weights, ceilings)
        peak_vals = jnp.maximum(peak_vals, jnp.where(active_tick, maxima, 0.0))
        saved_state = kept_state
        if stash is None:
            stash = jax.tree.map(
                lambda template: jnp.zeros((MICRO,) + template.shape, template.dtype), saved_state
            )
        stash = store_slot(stash, saved_state, slot_index, active_tick)
        outputs = store_rows(outputs, layer_out, slot_index * block_rows, active_tick)
        if moment + 1 < tick_count:
            incoming = from_behind(layer_out, "pipe", 1)
    pending = jnp.zeros_like(incoming)
    grad_inputs = jnp.zeros(tokens.shape, jnp.bfloat16)
    totals = None
    for moment in range(tick_count):
        micro_id = moment - (section_count - 1 - section_index)
        active_tick = (micro_id >= 0) & (micro_id < MICRO)
        slot_index = jnp.clip(micro_id, 0, MICRO - 1)
        first_row = min(moment, MICRO - 1) * block_rows
        row_lengths = lax.dynamic_slice_in_dim(lengths, slot_index * block_rows, block_rows)
        valid_mask = (jnp.arange(seq_len)[None, :] < row_lengths[:, None]).astype(jnp.bfloat16)
        seed_grad = cotangent[first_row : first_row + block_rows] * valid_mask[..., None]
        grad_out = jnp.where(is_last, seed_grad, pending)
        saved_state = jax.tree.map(
            lambda whole_buf: lax.dynamic_index_in_dim(whole_buf, slot_index, 0, keepdims=False),
            stash,
        )
        kept_state = saved_state
        grad_in, tick_grads = layer_backward(kept_state, grad_out, row_lengths, weights, ceilings)
        tick_grads = tuple((jnp.where(active_tick, grad_part, 0.0) for grad_part in tick_grads))
        totals = (
            tick_grads
            if totals is None
            else tuple((left_op + right_op for left_op, right_op in zip(totals, tick_grads)))
        )
        grad_inputs = store_rows(grad_inputs, grad_in, slot_index * block_rows, active_tick)
        if moment + 1 < tick_count:
            pending = from_behind(grad_in, "pipe", -1)
    totals = (
        lax.psum_scatter(totals[0], "dp", scatter_dimension=0, tiled=True),
        lax.psum_scatter(totals[1], "dp", scatter_dimension=0, tiled=True),
        lax.psum_scatter(totals[2], "dp", scatter_dimension=0, tiled=True),
        lax.psum_scatter(totals[3], "dp", scatter_dimension=0, tiled=True),
        lax.psum_scatter(totals[4], "dp", scatter_dimension=0, tiled=True),
        lax.psum_scatter(totals[5], "dp", scatter_dimension=0, tiled=True),
        lax.psum_scatter(totals[6], "dp", scatter_dimension=0, tiled=True),
        lax.psum_scatter(totals[7], "dp", scatter_dimension=0, tiled=True),
        lax.psum_scatter(totals[8], "dp", scatter_dimension=1, tiled=True),
        lax.psum_scatter(totals[9], "dp", scatter_dimension=1, tiled=True),
    )
    peak_all = lax.pmax(peak_vals, "dp")
    end_parts = (
        lax.psum_scatter(
            jnp.where(is_last, outputs, 0.0).astype(jnp.float32).astype(jnp.bfloat16),
            "pipe",
            scatter_dimension=1,
            tiled=True,
        ).astype(jnp.float32),
        lax.psum_scatter(
            jnp.where(is_first, grad_inputs, 0.0).astype(jnp.float32).astype(jnp.bfloat16),
            "pipe",
            scatter_dimension=1,
            tiled=True,
        ).astype(jnp.float32),
    )
    mixed = end_parts[0].astype(jnp.bfloat16)
    grad_tokens = end_parts[1].astype(jnp.bfloat16)
    layer_grads = tuple((grad_part[None] for grad_part in totals))
    batch_max = peak_all[None]
    return (mixed, grad_tokens) + layer_grads + (batch_max,)


def solution(mesh):
    return jax.shard_map(
        shards,
        mesh=mesh,
        in_specs=(
            P("dp", None, None),
            P("dp"),
            P("pipe", None),
            P("pipe", None, None),
            P("pipe", None),
            P("pipe", None, None),
            P("pipe", None),
            P("pipe", None, None),
            P("pipe", None),
            P("pipe", None, None),
            P("pipe", None),
            P("pipe", None, None),
            P("pipe", None, None),
            P("dp", None, None),
        ),
        out_specs=(
            P("dp", "pipe", None),
            P("dp", "pipe", None),
            P("pipe", "dp", None),
            P("pipe", "dp"),
            P("pipe", "dp", None),
            P("pipe", "dp"),
            P("pipe", "dp", None),
            P("pipe", "dp"),
            P("pipe", "dp", None),
            P("pipe", "dp"),
            P("pipe", None, "dp"),
            P("pipe", None, "dp"),
            P("pipe", None),
        ),
        check_vma=False,
    )
```

profile of v0, /device:TPU:0, one launch (start us, length us, event | category | flops | bytes accessed | tf_op | source)
XLA Modules:
  0.0 2189.1 jit_solution(15283700514905098827)
XLA Ops:
  58.1 20.2 select_reduce_fusion.6
  142.2 11.5 broadcast_in_dim.1082
  153.8 6.6 bitcast_dynamic-update-slice_fusion.6
  166.8 6.3 constant_dynamic-slice_fusion.87
  203.7 20.5 select_reduce_fusion.5
  258.4 9.2 bitcast_dynamic-update-slice_fusion.5
  309.9 20.2 select_reduce_fusion.4
  361.8 9.2 bitcast_dynamic-update-slice_fusion.4
  373.8 6.3 constant_dynamic-slice_fusion.85
  410.9 20.2 select_reduce_fusion.3
  462.7 9.4 bitcast_dynamic-update-slice_fusion.3
  474.9 6.4 constant_dynamic-slice_fusion.84
  512.9 23.1 %select_reduce_fusion.2 = (f32[]{:T(128)}, f32[512,3072]{1,0:T(8,128)S(1)}, f32[512,3072]{1,0:T(8,128)}) fusion(pred[512]{0:T(512)(128)(4,1)S(1)} %copy-done.407, f32[3072]{0:T(1024)S(1)} %bitcast.2531, bf16[1,768,3072]{2,1,0:T(8,128)(2,1)} %param.21, f32[768]{0:T(1024)S(1)} %get-tuple-element.420, f32[768]{0:T(1024)S(1)} %get-tuple-element.410, ...), kind=kOutput, calls=%fused_computation.242 | convolution fusion | flops 2525626368 | bytes 18897416 | tf_op jit(solution)/shard_map/rsd,de->rse/dot_general | solution.py:38
  579.6 9.2 bitcast_dynamic-update-slice_fusion.2
  628.1 23.0 %select_reduce_fusion.1 = (f32[]{:T(128)}, f32[512,3072]{1,0:T(8,128)S(1)}, f32[512,3072]{1,0:T(8,128)}) fusion(pred[512]{0:T(512)(128)(4,1)S(1)} %copy-done.444, f32[3072]{0:T(1024)S(1)} %bitcast.2533, bf16[1,768,3072]{2,1,0:T(8,128)(2,1)} %param.21, f32[768]{0:T(1024)S(1)} %get-tuple-element.420, f32[768]{0:T(1024)S(1)} %get-tuple-element.410, ...), kind=kOutput, calls=%fused_computation.241 | convolution fusion | flops 2525626368 | bytes 18897416 | tf_op jit(solution)/shard_map/rsd,de->rse/dot_general | solution.py:38
  686.3 9.2 bitcast_dynamic-update-slice_fusion.1
  698.3 6.3 constant_dynamic-slice_fusion.82
  735.1 20.2 select_reduce_fusion
  785.8 7.0 bitcast_dynamic-update-slice_fusion
  792.8 21.3 convert_reduce_fusion.6
  814.1 8.1 multiply_reduce_fusion.13
  831.7 8.7 constant_dynamic-slice_fusion.18
  861.9 7.4 multiply_reduce_fusion.6
  869.3 7.2 multiply_convert_fusion.6
  929.0 7.8 fusion.932
  943.3 21.6 convert_reduce_fusion.5
  979.0 7.8 fusion.587
  986.9 11.6 multiply_reduce_fusion.5
  999.7 7.5 multiply_convert_fusion.5
  1019.1 6.3 fusion.933
  1029.7 22.4 %convert_reduce_fusion.4 = (f32[3072]{0:T(1024)}, bf16[512,3072]{1,0:T(8,128)(2,1)S(1)}) fusion(f32[]{:T(128)} %bitcast.13, bf16[1,3072,768]{2,1,0:T(8,128)(2,1)S(1)} %bitcast.2559, bf16[1,512,768]{2,1,0:T(8,128)(2,1)S(1)} %get-tuple-element.461, f32[4,1,512,3072]{3,2,1,0:T(8,128)} %bitcast_dynamic-update-slice_fusion, s32[]{:T(128)S(6)} %min.52), kind=kOutput, calls=%fused_computation.251 | convolution fusion | flops 2540172288 | bytes 14954504 | tf_op jit(solution)/shard_map/rse,de->rsd/dot_general | solution.py:42
  1066.3 7.8 fusion.590
  1074.2 11.6 multiply_reduce_fusion.4
  1087.0 7.3 multiply_convert_fusion.4
  1118.4 22.4 %convert_reduce_fusion.3 = (f32[3072]{0:T(1024)}, bf16[512,3072]{1,0:T(8,128)(2,1)S(1)}) fusion(f32[]{:T(128)} %bitcast.13, bf16[1,3072,768]{2,1,0:T(8,128)(2,1)S(1)} %bitcast.2561, bf16[1,512,768]{2,1,0:T(8,128)(2,1)S(1)} %get-tuple-element.463, f32[4,1,512,3072]{3,2,1,0:T(8,128)} %bitcast_dynamic-update-slice_fusion, s32[]{:T(128)S(6)} %min.53), kind=kOutput, calls=%fused_computation.250 | convolution fusion | flops 2540172288 | bytes 14954504 | tf_op jit(solution)/shard_map/rse,de->rsd/dot_general | solution.py:42
  1154.9 7.8 fusion.593
  1162.7 11.6 multiply_reduce_fusion.3
  1175.6 7.3 multiply_convert_fusion.3
  1194.7 6.3 fusion.935
  1210.4 22.4 %convert_reduce_fusion.2 = (f32[3072]{0:T(1024)}, bf16[512,3072]{1,0:T(8,128)(2,1)S(1)}) fusion(f32[]{:T(128)} %bitcast.13, bf16[1,3072,768]{2,1,0:T(8,128)(2,1)S(1)} %bitcast.2563, bf16[1,512,768]{2,1,0:T(8,128)(2,1)S(1)} %get-tuple-element.465, f32[4,1,512,3072]{3,2,1,0:T(8,128)} %bitcast_dynamic-update-slice_fusion, s32[]{:T(128)S(6)} %min.54), kind=kOutput, calls=%fused_computation.249 | convolution fusion | flops 2540172288 | bytes 14954504 | tf_op jit(solution)/shard_map/rse,de->rsd/dot_general | solution.py:42
  1247.0 7.8 fusion.596
  1254.9 11.6 multiply_reduce_fusion.2
  1267.7 7.5 multiply_convert_fusion.2
  1302.6 22.4 %convert_reduce_fusion.1 = (f32[3072]{0:T(1024)}, bf16[512,3072]{1,0:T(8,128)(2,1)S(1)}) fusion(f32[]{:T(128)} %bitcast.13, bf16[1,3072,768]{2,1,0:T(8,128)(2,1)S(1)} %bitcast.2565, bf16[1,512,768]{2,1,0:T(8,128)(2,1)S(1)} %get-tuple-element.467, f32[4,1,512,3072]{3,2,1,0:T(8,128)} %bitcast_dynamic-update-slice_fusion, s32[]{:T(128)S(6)} %min.55), kind=kOutput, calls=%fused_computation.248 | convolution fusion | flops 2540172288 | bytes 14954504 | tf_op jit(solution)/shard_map/rse,de->rsd/dot_general | solution.py:42
  1339.2 7.8 fusion.599
  1347.0 11.6 multiply_reduce_fusion.1
  1359.9 7.3 multiply_convert_fusion.1
  1394.2 21.2 convert_reduce_fusion
  1415.5 7.4 multiply_reduce_fusion.7
  1458.4 6.3 fusion.937
  1493.0 6.3 select_add_fusion.3
  1499.6 11.8 multiply_reduce_fusion
  1512.7 7.2 multiply_convert_fusion
  1535.7 7.0 fusion.670
  1568.0 15.0 select_add_fusion.2
  1625.1 16.9 select_add_fusion.1
  1648.5 6.4 bitcast_dynamic-update-slice_fusion.13
  1690.9 8.7 fusion.382
  1725.2 16.5 select_add_fusion
  1790.3 17.5 fusion.815
  1808.5 23.0 %pmax.7 = f32[1,4]{1,0:T(1,128)} all-reduce(f32[1,4]{1,0:T(1,128)S(1)} %fusion.815), channel_id=1, replica_groups=mesh['dp'=8,'pipe'=4] {'dp'}, use_global_device_ids=true, to_apply=%region_208.209 | all-reduce | flops 4 | bytes 32 | tf_op jit(solution)/shard_map/pmax | solution.py:332
  1840.9 35.0 %all-reduce.4 = (f32[1536]{0:T(1024)}, f32[768]{0:T(1024)}, f32[3072]{0:T(1024)}, f32[768]{0:T(1024)}) all-reduce(f32[1536]{0:T(1024)} %fusion.781, f32[768]{0:T(1024)S(1)} %select_add_fusion.6, f32[3072]{0:T(1024)S(1)} %select_add_fusion.4, f32[768]{0:T(1024)} %select_add_fusion.5), channel_id=5, replica_groups=mesh['dp'=8,'pipe'=4] {'dp'}, use_global_device_ids=true, to_apply=%region_122.123.clone | all-reduce | flops 6144 | bytes 49152
  1883.9 131.0 %reduce-scatter.21.cloned.1.call-done = f32[96,3072]{1,0:T(8,128)} async-done(((f32[768,3072]{1,0:T(8,128)}), f32[96,3072]{1,0:T(8,128)}) %reduce-scatter.21.cloned.1.call-update) | async-done | bytes 1179664 | tf_op jit(solution)/shard_map/reduce_scatter | solution.py:325
  2014.9 167.2 %reduce-scatter.23.cloned.1.call-done = f32[384,768]{1,0:T(8,128)} async-done(((f32[3072,768]{1,0:T(8,128)}), f32[384,768]{1,0:T(8,128)}) %reduce-scatter.23.cloned.1.call-update) | async-done | bytes 1179664 | tf_op jit(solution)/shard_map/reduce_scatter | solution.py:327
  (1840 shorter events, 1098.9 us)
Async XLA Ops:
  7.2 1873.8 %reduce-scatter.25.cloned.1.call-start = ((), (), s32[]{:S(2)}) async-start(), calls=%async_computation.14 | async-start | bytes 442368
  8.7 805.3 %copy-start.269 = (f32[768]{0:T(1024)}, f32[768]{0:T(1024)S(1)}, u32[]{:S(2)}) copy-start(f32[768]{0:T(1024)S(1)} %get-tuple-element.420) | copy-start | bytes 9220
  9.5 774.5 %copy-start.210 = (f32[768]{0:T(1024)}, f32[768]{0:T(1024)S(1)}, u32[]{:S(2)}) copy-start(f32[768]{0:T(1024)S(1)} %get-tuple-element.409) | copy-start | bytes 9220
  9.5 812.7 %copy-start.218 = (f32[768]{0:T(1024)}, f32[768]{0:T(1024)S(1)}, u32[]{:S(2)}) copy-start(f32[768]{0:T(1024)S(1)} %get-tuple-element.410) | copy-start | bytes 9220
  55.4 22.9 %slice-start.54 = ((s8[4718592]{0:T(1024)(128)(4,1)}), s8[4194304]{0:T(1024)(128)(4,1)S(1)}, s32[]{:S(2)}) async-start(s8[4718592]{0:T(1024)(128)(4,1)} %bitcast.2542), calls=%async_computation.70 | async-start | bytes 8388608
  85.7 87.4 %collective-permute-start = (bf16[1,512,768]{2,1,0:T(8,128)(2,1)}, bf16[1,512,768]{2,1,0:T(8,128)(2,1)}, u32[]{:S(2)}, u32[]{:S(2)}) collective-permute-start(bf16[1,512,768]{2,1,0:T(8,128)(2,1)} %get-tuple-element.583), channel_id=1, source_target_pairs={{0,1},{1,2},{2,3},{4,5},{5,6},{6,7},{8,9},{9,10},{10,11},{12,13},{... | collective-permute-start | bytes 2359304 | tf_op jit(solution)/shard_map/ppermute | solution.py:19
  235.1 44.3 %collective-permute-start.1 = (bf16[1,512,768]{2,1,0:T(8,128)(2,1)}, bf16[1,512,768]{2,1,0:T(8,128)(2,1)}, u32[]{:S(2)}, u32[]{:S(2)}) collective-permute-start(bf16[1,512,768]{2,1,0:T(8,128)(2,1)} %get-tuple-element.581), channel_id=1, source_target_pairs={{0,1},{1,2},{2,3},{4,5},{5,6},{6,7},{8,9},{9,10},{10,11},{12,13},{... | collective-permute-start | bytes 2359304 | tf_op jit(solution)/shard_map/ppermute | solution.py:19
  341.1 39.0 %collective-permute-start.2 = (bf16[1,512,768]{2,1,0:T(8,128)(2,1)}, bf16[1,512,768]{2,1,0:T(8,128)(2,1)}, u32[]{:S(2)}, u32[]{:S(2)}) collective-permute-start(bf16[1,512,768]{2,1,0:T(8,128)(2,1)} %get-tuple-element.579), channel_id=1, source_target_pairs={{0,1},{1,2},{2,3},{4,5},{5,6},{6,7},{8,9},{9,10},{10,11},{12,13},{... | collective-permute-start | bytes 2359304 | tf_op jit(solution)/shard_map/ppermute | solution.py:19
  442.0 39.2 %collective-permute-start.3 = (bf16[1,512,768]{2,1,0:T(8,128)(2,1)}, bf16[1,512,768]{2,1,0:T(8,128)(2,1)}, u32[]{:S(2)}, u32[]{:S(2)}) collective-permute-start(bf16[1,512,768]{2,1,0:T(8,128)(2,1)} %get-tuple-element.577), channel_id=1, source_target_pairs={{0,1},{1,2},{2,3},{4,5},{5,6},{6,7},{8,9},{9,10},{10,11},{12,13},{... | collective-permute-start | bytes 2359304 | tf_op jit(solution)/shard_map/ppermute | solution.py:19
  511.6 24.4 %slice-start.62 = ((s8[4718592]{0:T(1024)(128)(4,1)}), s8[4194304]{0:T(1024)(128)(4,1)S(1)}, s32[]{:S(2)}) async-start(s8[4718592]{0:T(1024)(128)(4,1)} %bitcast.2550), calls=%async_computation.78 | async-start | bytes 8388608
  512.5 23.4 %copy-start.12 = (f32[1,512,768]{2,1,0:T(8,128)}, f32[1,512,768]{2,1,0:T(8,128)S(1)}, u32[]{:S(2)}) copy-start(f32[1,512,768]{2,1,0:T(8,128)S(1)} %get-tuple-element.706) | copy-start | bytes 4718596
  512.5 23.4 %copy-start.338 = (f32[512]{0:T(512)}, f32[512]{0:T(512)S(1)}, u32[]{:S(2)}) copy-start(f32[512]{0:T(512)S(1)} %broadcast_multiply_fusion.19) | copy-start | bytes 6148
  512.9 23.1 %copy-start.367 = (f32[512]{0:T(512)}, f32[512]{0:T(512)S(1)}, u32[]{:S(2)}) copy-start(f32[512]{0:T(512)S(1)} %add_rsqrt_fusion.5) | copy-start | bytes 6148
  512.9 23.1 %copy-start.463 = (f32[768]{0:T(1024)S(1)}, f32[768]{0:T(1024)}, u32[]{:S(2)}) copy-start(f32[768]{0:T(1024)} %reduce.159) | copy-start | bytes 9220
  512.9 23.1 %slice-start.63 = ((s8[4718592]{0:T(1024)(128)(4,1)}), s8[524288]{0:T(1024)(128)(4,1)S(1)}, s32[]{:S(2)}) async-start(s8[4718592]{0:T(1024)(128)(4,1)} %bitcast.2550), calls=%async_computation.79 | async-start | bytes 1048576
  546.8 51.1 %collective-permute-start.4 = (bf16[1,512,768]{2,1,0:T(8,128)(2,1)}, bf16[1,512,768]{2,1,0:T(8,128)(2,1)}, u32[]{:S(2)}, u32[]{:S(2)}) collective-permute-start(bf16[1,512,768]{2,1,0:T(8,128)(2,1)} %get-tuple-element.575), channel_id=1, source_target_pairs={{0,1},{1,2},{2,3},{4,5},{5,6},{6,7},{8,9},{9,10},{10,11},{12,13},{... | collective-permute-start | bytes 2359304 | tf_op jit(solution)/shard_map/ppermute | solution.py:19
  626.8 24.3 %slice-start.64 = ((s8[4718592]{0:T(1024)(128)(4,1)}), s8[4194304]{0:T(1024)(128)(4,1)S(1)}, s32[]{:S(2)}) async-start(s8[4718592]{0:T(1024)(128)(4,1)} %bitcast.2552), calls=%async_computation.80 | async-start | bytes 8388608
  627.7 23.4 %copy-start.14 = (f32[1,512,768]{2,1,0:T(8,128)}, f32[1,512,768]{2,1,0:T(8,128)S(1)}, u32[]{:S(2)}) copy-start(f32[1,512,768]{2,1,0:T(8,128)S(1)} %get-tuple-element.714) | copy-start | bytes 4718596
  627.8 23.3 %copy-start.341 = (f32[512]{0:T(512)}, f32[512]{0:T(512)S(1)}, u32[]{:S(2)}) copy-start(f32[512]{0:T(512)S(1)} %broadcast_multiply_fusion.17) | copy-start | bytes 6148
  628.1 23.0 %copy-start.369 = (f32[512]{0:T(512)}, f32[512]{0:T(512)S(1)}, u32[]{:S(2)}) copy-start(f32[512]{0:T(512)S(1)} %add_rsqrt_fusion.3) | copy-start | bytes 6148
  628.1 23.0 %copy-start.464 = (f32[768]{0:T(1024)S(1)}, f32[768]{0:T(1024)}, u32[]{:S(2)}) copy-start(f32[768]{0:T(1024)} %reduce.159) | copy-start | bytes 9220
  628.1 23.0 %slice-start.65 = ((s8[4718592]{0:T(1024)(128)(4,1)}), s8[524288]{0:T(1024)(128)(4,1)S(1)}, s32[]{:S(2)}) async-start(s8[4718592]{0:T(1024)(128)(4,1)} %bitcast.2552), calls=%async_computation.81 | async-start | bytes 1048576
  662.1 42.5 %collective-permute-start.5 = (bf16[1,512,768]{2,1,0:T(8,128)(2,1)}, bf16[1,512,768]{2,1,0:T(8,128)(2,1)}, u32[]{:S(2)}, u32[]{:S(2)}) collective-permute-start(bf16[1,512,768]{2,1,0:T(8,128)(2,1)} %get-tuple-element.573), channel_id=1, source_target_pairs={{0,1},{1,2},{2,3},{4,5},{5,6},{6,7},{8,9},{9,10},{10,11},{12,13},{... | collective-permute-start | bytes 2359304 | tf_op jit(solution)/shard_map/ppermute | solution.py:19
  784.9 29.2 %copy-start.427 = (f32[512]{0:T(512)}, f32[512]{0:T(512)S(1)}, u32[]{:S(2)}) copy-start(f32[512]{0:T(512)S(1)} %get-tuple-element.786) | copy-start | bytes 6148
  784.9 29.2 %copy-start.429 = (f32[512]{0:T(512)}, f32[512]{0:T(512)S(1)}, u32[]{:S(2)}) copy-start(f32[512]{0:T(512)S(1)} %get-tuple-element.787) | copy-start | bytes 6148
  784.9 29.2 %copy-start.423 = (f32[512]{0:T(512)}, f32[512]{0:T(512)S(1)}, u32[]{:S(2)}) copy-start(f32[512]{0:T(512)S(1)} %get-tuple-element.784) | copy-start | bytes 6148
  784.9 29.2 %copy-start.425 = (f32[512]{0:T(512)}, f32[512]{0:T(512)S(1)}, u32[]{:S(2)}) copy-start(f32[512]{0:T(512)S(1)} %get-tuple-element.785) | copy-start | bytes 6148
  784.9 29.1 %copy-start.418 = (f32[512]{0:T(512)}, f32[512]{0:T(512)S(1)}, u32[]{:S(2)}) copy-start(f32[512]{0:T(512)S(1)} %get-tuple-element.782) | copy-start | bytes 6148
  785.0 29.1 %copy-start.421 = (f32[512]{0:T(512)}, f32[512]{0:T(512)S(1)}, u32[]{:S(2)}) copy-start(f32[512]{0:T(512)S(1)} %get-tuple-element.783) | copy-start | bytes 6148
  822.2 60.1 %copy-start.439 = (f32[512]{0:T(512)}, f32[512]{0:T(512)S(1)}, u32[]{:S(2)}) copy-start(f32[512]{0:T(512)S(1)} %get-tuple-element.292) | copy-start | bytes 6148
  889.2 47.5 %collective-permute-start.6 = (bf16[1,512,768]{2,1,0:T(8,128)(2,1)}, bf16[1,512,768]{2,1,0:T(8,128)(2,1)}, u32[]{:S(2)}, u32[]{:S(2)}) collective-permute-start(bf16[1,512,768]{2,1,0:T(8,128)(2,1)} %get-tuple-element.730), channel_id=1, source_target_pairs={{1,0},{2,1},{3,2},{5,4},{6,5},{7,6},{9,8},{10,9},{11,10},{13,12},{... | collective-permute-start | bytes 2359304 | tf_op jit(solution)/shard_map/ppermute | solution.py:19
  940.2 24.7 %slice-start.12 = ((s8[6291456]{0:T(1024)(128)(4,1)}), s8[4194304]{0:T(1024)(128)(4,1)S(1)}, s32[]{:S(2)}) async-start(s8[6291456]{0:T(1024)(128)(4,1)} %bitcast.2337), calls=%async_computation.28 | async-start | bytes 8388608
  940.2 24.7 %slice-start.88 = ((s8[4718592]{0:T(1024)(128)(4,1)}), s8[4194304]{0:T(1024)(128)(4,1)S(1)}, s32[]{:S(2)}) async-start(s8[4718592]{0:T(1024)(128)(4,1)} %bitcast.2576), calls=%async_computation.104 | async-start | bytes 8388608
  986.8 23.7 %copy-start.221 = (bf16[12,64,512]{2,1,0:T(8,128)(2,1)}, bf16[12,64,512]{2,1,0:T(8,128)(2,1)S(1)}, u32[]{:S(2)}) copy-start(bf16[12,64,512]{2,1,0:T(8,128)(2,1)S(1)} %fusion.587) | copy-start | bytes 2359300
  1017.1 8.2 collective-permute-start.7
  1028.2 24.0 %slice-start.14 = ((s8[6291456]{0:T(1024)(128)(4,1)}), s8[2097152]{0:T(1024)(128)(4,1)S(1)}, s32[]{:S(2)}) async-start(s8[6291456]{0:T(1024)(128)(4,1)} %bitcast.2339), calls=%async_computation.30 | async-start | bytes 4194304
  1028.2 23.9 %slice-start.90 = ((s8[4718592]{0:T(1024)(128)(4,1)}), s8[4194304]{0:T(1024)(128)(4,1)S(1)}, s32[]{:S(2)}) async-start(s8[4718592]{0:T(1024)(128)(4,1)} %bitcast.2578), calls=%async_computation.106 | async-start | bytes 8388608
  1074.1 23.5 %copy-start.224 = (bf16[12,64,512]{2,1,0:T(8,128)(2,1)}, bf16[12,64,512]{2,1,0:T(8,128)(2,1)S(1)}, u32[]{:S(2)}) copy-start(bf16[12,64,512]{2,1,0:T(8,128)(2,1)S(1)} %fusion.590) | copy-start | bytes 2359300
  1104.2 9.8 collective-permute-start.8
  1116.8 24.0 %slice-start.16 = ((s8[6291456]{0:T(1024)(128)(4,1)}), s8[2097152]{0:T(1024)(128)(4,1)S(1)}, s32[]{:S(2)}) async-start(s8[6291456]{0:T(1024)(128)(4,1)} %bitcast.2341), calls=%async_computation.32 | async-start | bytes 4194304
  1116.8 23.9 %slice-start.92 = ((s8[4718592]{0:T(1024)(128)(4,1)}), s8[4194304]{0:T(1024)(128)(4,1)S(1)}, s32[]{:S(2)}) async-start(s8[4718592]{0:T(1024)(128)(4,1)} %bitcast.2580), calls=%async_computation.108 | async-start | bytes 8388608
  1162.7 23.5 %copy-start.227 = (bf16[12,64,512]{2,1,0:T(8,128)(2,1)}, bf16[12,64,512]{2,1,0:T(8,128)(2,1)S(1)}, u32[]{:S(2)}) copy-start(bf16[12,64,512]{2,1,0:T(8,128)(2,1)S(1)} %fusion.593) | copy-start | bytes 2359300
  1192.8 13.3 collective-permute-start.9
  1208.9 24.0 %slice-start.18 = ((s8[6291456]{0:T(1024)(128)(4,1)}), s8[2097152]{0:T(1024)(128)(4,1)S(1)}, s32[]{:S(2)}) async-start(s8[6291456]{0:T(1024)(128)(4,1)} %bitcast.2343), calls=%async_computation.34 | async-start | bytes 4194304
  1208.9 24.0 %slice-start.94 = ((s8[4718592]{0:T(1024)(128)(4,1)}), s8[4194304]{0:T(1024)(128)(4,1)S(1)}, s32[]{:S(2)}) async-start(s8[4718592]{0:T(1024)(128)(4,1)} %bitcast.2582), calls=%async_computation.110 | async-start | bytes 8388608
  1254.8 23.6 %copy-start.230 = (bf16[12,64,512]{2,1,0:T(8,128)(2,1)}, bf16[12,64,512]{2,1,0:T(8,128)(2,1)S(1)}, u32[]{:S(2)}) copy-start(bf16[12,64,512]{2,1,0:T(8,128)(2,1)S(1)} %fusion.596) | copy-start | bytes 2359300
  1285.0 13.3 collective-permute-start.10
  1301.1 24.0 %slice-start.20 = ((s8[6291456]{0:T(1024)(128)(4,1)}), s8[2097152]{0:T(1024)(128)(4,1)S(1)}, s32[]{:S(2)}) async-start(s8[6291456]{0:T(1024)(128)(4,1)} %bitcast.2345), calls=%async_computation.36 | async-start | bytes 4194304
  1301.1 24.0 %slice-start.96 = ((s8[4718592]{0:T(1024)(128)(4,1)}), s8[4194304]{0:T(1024)(128)(4,1)S(1)}, s32[]{:S(2)}) async-start(s8[4718592]{0:T(1024)(128)(4,1)} %bitcast.2584), calls=%async_computation.112 | async-start | bytes 8388608
  1302.6 22.5 %slice-start.21 = ((s8[6291456]{0:T(1024)(128)(4,1)}), s8[4194304]{0:T(1024)(128)(4,1)S(1)}, s32[]{:S(2)}) async-start(s8[6291456]{0:T(1024)(128)(4,1)} %bitcast.2345), calls=%async_computation.37 | async-start | bytes 8388608
  1302.6 22.5 %copy-start.417 = (f32[512]{0:T(512)S(1)}, f32[512]{0:T(512)}, u32[]{:S(2)}) copy-start(f32[512]{0:T(512)} %fusion.805) | copy-start | bytes 6148
  1302.6 22.5 %copy-start.422 = (f32[512]{0:T(512)S(1)}, f32[512]{0:T(512)}, u32[]{:S(2)}) copy-start(f32[512]{0:T(512)} %copy-done.421) | copy-start | bytes 6148
  1302.6 22.5 %slice-start.97 = ((s8[4718592]{0:T(1024)(128)(4,1)}), s8[524288]{0:T(1024)(128)(4,1)S(1)}, s32[]{:S(2)}) async-start(s8[4718592]{0:T(1024)(128)(4,1)} %bitcast.2584), calls=%async_computation.113 | async-start | bytes 1048576
  1347.0 23.5 %copy-start.233 = (bf16[12,64,512]{2,1,0:T(8,128)(2,1)}, bf16[12,64,512]{2,1,0:T(8,128)(2,1)S(1)}, u32[]{:S(2)}) copy-start(bf16[12,64,512]{2,1,0:T(8,128)(2,1)S(1)} %fusion.599) | copy-start | bytes 2359300
  1377.2 13.3 collective-permute-start.11
  1379.8 35.6 %copy-start.413 = (f32[512]{0:T(512)}, f32[512]{0:T(512)S(1)}, u32[]{:S(2)}) copy-start(f32[512]{0:T(512)S(1)} %fusion.807) | copy-start | bytes 6148
  1392.7 22.7 %slice-start.98 = ((s8[4718592]{0:T(1024)(128)(4,1)}), s8[4194304]{0:T(1024)(128)(4,1)S(1)}, s32[]{:S(2)}) async-start(s8[4718592]{0:T(1024)(128)(4,1)} %bitcast.2586), calls=%async_computation.114 | async-start | bytes 8388608
  1425.2 457.3 %reduce-scatter.27.cloned.1.call-start = ((), (), s32[]{:S(2)}) async-start(), calls=%async_computation.15 | async-start | bytes 442368
  1429.0 454.9 %reduce-scatter.13.cloned.1.call-start = ((), (), s32[]{:S(2)}) async-start(), calls=%async_computation.8 | async-start | bytes 3932160 | tf_op jit(solution)/shard_map/reduce_scatter | solution.py:334
  1430.9 453.0 %reduce-scatter.19.cloned.1.call-start = ((), (), s32[]{:S(2)}) async-start(), calls=%async_computation.11 | async-start | bytes 2654208 | tf_op jit(solution)/shard_map/reduce_scatter | solution.py:323
  1499.3 384.6 %reduce-scatter.15.cloned.1.call-start = ((), (), s32[]{:S(2)}) async-start(), calls=%async_computation.9 | async-start | bytes 3932160 | tf_op jit(solution)/shard_map/reduce_scatter | solution.py:340
  1535.4 348.5 %reduce-scatter.17.cloned.1.call-start = ((), (), s32[]{:S(2)}) async-start(), calls=%async_computation.10 | async-start | bytes 7962624 | tf_op jit(solution)/shard_map/reduce_scatter | solution.py:321
  1583.0 431.9 %reduce-scatter.21.cloned.1.call-start = ((), (), s32[]{:S(2)}) async-start(), calls=%async_computation.12 | async-start | bytes 10616832 | tf_op jit(solution)/shard_map/reduce_scatter | solution.py:325
  1642.1 540.0 %reduce-scatter.23.cloned.1.call-start = ((), (), s32[]{:S(2)}) async-start(), calls=%async_computation.13 | async-start | bytes 10616832 | tf_op jit(solution)/shard_map/reduce_scatter | solution.py:327
  (558 other events, 4299.7 us)
Sparse Core Ops, SparseCore 0:
  1425.3 70.9 reduce-scatter.24
  1499.6 60.3 reduce-scatter.26
  1563.1 36.9 reduce-scatter.12
  1604.4 68.9 reduce-scatter.18
  1676.6 37.0 reduce-scatter.14
  1717.7 129.2 reduce-scatter.16
  1851.6 163.2 reduce-scatter.20
  2019.5 162.5 reduce-scatter.22
where the time goes:
time: 2200 us; the launch traced here: 2190 us
  matrix products  891 us (40%)
  other arithmetic  450 us (20%)
  local copies, waits for them, and re-layouts  426 us (19%)
  waiting for transfers between devices  313 us (14%)
  blocking collectives  57.9 us (3%)
  starting transfers between devices  28 us (1%)
  between operations  23.4 us (1%)
    dot_general x28, matrix products, matmul_back(): jnp.einsum('rse,de->rsd', left_op, right_op, preferred_element_type=jnp.f...  258 us
    dynamic_update_slice x75, other arithmetic, place_one(): lax.dynamic_update_index_in_dim(whole_buf, jnp.where(active_tick, new_pie...  218 us
    dot_general x28, matrix products, matmul(): jnp.einsum('rsd,de->rse', left_op, right_op, preferred_element_type=jnp.f...  203 us
    dot_general x28, matrix products, weight_grad(): jnp.einsum('rsd,rse->de', left_op, right_op, preferred_element_type=jnp.f...  173 us
    reduce_scatter x1, waiting for transfers between devices, shards(): lax.psum_scatter(totals[6], 'dp', scatter_dimension=0, tiled=True)  167 us
    dynamic_slice x60, local copies, waits for them, and re-layouts, place_one(): lax.dynamic_index_in_dim(whole_buf, slot_index, 0, keepdims=False)  139 us
    reduce_scatter x1, waiting for transfers between devices, shards(): lax.psum_scatter(totals[4], 'dp', scatter_dimension=0, tiled=True)  131 us
    dot_general x7, matrix products, attend_back(): jnp.einsum('qhd,khd->hqk', grad_heads, split_heads(values_low), preferred...  77.4 us
  transfers between devices with their start and end apart: 20, of which 6 were waited for; matrix products, arithmetic and copies ran while one was open for 34% of the time, Pallas kernels for 0%

commit v1 on v0

v1 whole, which is shorter than its diff:
```python
import jax
import jax.numpy as jnp
from jax import lax
from jax.experimental import pallas as pl
from jax.experimental.pallas import tpu as pltpu
from jax.sharding import PartitionSpec as P

HEAD_DIM = 64
PAIR = 2 * HEAD_DIM
EPS = 1e-06
MASKED = -1000000000.0
CHUNK = 512
ROWS = 64
LOGICAL = pl.DeviceIdType.MESH
F32 = jnp.float32
BF16 = jnp.bfloat16

ERF_POLY = (
    0.7978846780398201,
    0.03633450830808018,
    -3.432973817348946e-05,
    -5.463434792182573e-05,
    3.860434711489827e-06,
    -1.254735264100511e-07,
    1.6084598007909267e-09,
)
ERF_CLAMP = 5.3 * 5.3
INV_SQRT_2PI = 0.3989422804014327


def dot_nn(a, b):
    return jnp.dot(a, b, preferred_element_type=F32)


def dot_nt(a, b):
    return lax.dot_general(a, b, (((1,), (1,)), ((), ())), preferred_element_type=F32)


def fold_rows(v):
    return jnp.sum(v.reshape(v.shape[0] // 8, 8, v.shape[1]), 0)


def peak_rows(v):
    tiles = [v[:, i : i + 128] for i in range(0, v.shape[1], 128)]
    top = tiles[0]
    for tile in tiles[1:]:
        top = jnp.maximum(top, tile)
    return jnp.max(top.reshape(v.shape[0] // 8, 8, 128), 0)


def split3(v):
    hi = v.astype(BF16)
    rest = v - hi.astype(F32)
    mid = rest.astype(BF16)
    low = (rest - mid.astype(F32)).astype(BF16)
    return hi, mid, low


def greet(stage, count):
    barrier = pltpu.get_barrier_semaphore()
    for step in range(1, count):
        peer = lax.rem(stage + step, count)
        pl.semaphore_signal(barrier, inc=1, device_id={"pipe": peer}, device_id_type=LOGICAL)
    pl.semaphore_wait(barrier, count - 1)


def activation(u, ceiling, inv_ceiling):
    w = jnp.minimum(u * u, ERF_CLAMP)
    poly = w * ERF_POLY[-1] + ERF_POLY[-2]
    for coef in ERF_POLY[-3::-1]:
        poly = poly * w + coef
    phi_cdf = 0.5 + 0.5 * jnp.tanh(u * poly)
    act = u * phi_cdf
    ratio = jnp.tanh(act * inv_ceiling)
    slope = (1.0 - ratio * ratio) * (
        phi_cdf + (u * INV_SQRT_2PI) * jnp.exp(u * u * -0.5)
    )
    return act, ceiling * ratio, slope


def fwd_kernel(count, *refs):
    (
        lens, scales, tokens, w_qkv, b_qkv, w_out, b_out, w_up, b_up, w_down, b_down, gain, shift,
        x_o, xq_o, qkv_o, lse_o, ctx_o, cq_o, n1_o, rs1_o, hq_o, aq_o, sl_o, n2_o, rs2_o,
        mixed_o, peaks_o,
        xin, xout, xq_s, qkv_s, lse_s, ctx_s, cq_s, n1_s, rs1_s, hq_s, aq_s, sl_s, n2_s, rs2_s,
        acc, hid, up_s, save_sem, in_sem, send_sem, recv_sem, mix_send, mix_recv,
    ) = refs
    r = pl.program_id(0)
    rows = pl.num_programs(0)
    row_count = tokens.shape[0]
    seq, width = tokens.shape[1], tokens.shape[2]
    ff = w_up.shape[1]
    piece = seq // count
    stage = lax.axis_index("pipe")
    first = stage == 0
    last = stage == count - 1

    staged = {
        "x": (xin.at[r], x_o), "xq": (xq_s, xq_o), "qkv": (qkv_s, qkv_o), "lse": (lse_s, lse_o),
        "ctx": (ctx_s, ctx_o), "cq": (cq_s, cq_o), "n1": (n1_s, n1_o), "rs1": (rs1_s, rs1_o),
        "hq": (hq_s, hq_o), "aq": (aq_s, aq_o), "sl": (sl_s, sl_o), "n2": (n2_s, n2_o),
        "rs2": (rs2_s, rs2_o),
    }
    order = list(staged)

    def save_copy(name):
        src, dst = staged[name]
        return pltpu.make_async_copy(src, dst.at[r], save_sem.at[order.index(name)])

    def save(name):
        save_copy(name).start()

    def reuse(*names):
        @pl.when(r > 0)
        def _():
            for name in names:
                save_copy(name).wait()

    def token_copy(i):
        return pltpu.make_async_copy(tokens.at[i], xin.at[i], in_sem.at[i])

    def hop(i):
        return pltpu.make_async_remote_copy(
            src_ref=xout.at[i], dst_ref=xin.at[i], send_sem=send_sem.at[i], recv_sem=recv_sem.at[i],
            device_id={"pipe": lax.rem(stage + 1, count)}, device_id_type=LOGICAL,
        )

    def mix_part(i, p):
        return pltpu.make_async_remote_copy(
            src_ref=xout.at[i, pl.ds(p * piece, piece)], dst_ref=mixed_o.at[i],
            send_sem=mix_send.at[i, p], recv_sem=mix_recv.at[i],
            device_id={"pipe": jnp.int32(p)}, device_id_type=LOGICAL,
        )

    def mix_own(i):
        return pltpu.make_async_copy(
            xout.at[i, pl.ds((count - 1) * piece, piece)], mixed_o.at[i], mix_send.at[i, count - 1]
        )

    @pl.when(r == 0)
    def _():
        greet(stage, count)
        peaks_o[...] = jnp.zeros_like(peaks_o)

        @pl.when(first)
        def _():
            for i in range(row_count):
                token_copy(i).start()

    @pl.when(first)
    def _():
        token_copy(r).wait()

    @pl.when(jnp.logical_not(first))
    def _():
        hop(r).wait_recv()

    length = lens[r]
    m0, m1, m2, m3 = scales[0, 0], scales[0, 1], scales[0, 2], scales[0, 3]
    i0, i1, i2, i3 = 1.0 / m0, 1.0 / m1, 1.0 / m2, 1.0 / m3
    steps = seq // ROWS

    def row_mask(start, size):
        return (start + lax.broadcasted_iota(jnp.int32, (size, 1), 0)) < length

    def note_peak(k, v, start):
        top = jnp.where(row_mask(start, v.shape[0]), jnp.abs(v), 0.0)
        peaks_o[k] = jnp.maximum(peaks_o[k], peak_rows(top))

    @pl.when(r > 0)
    def _():
        save_copy("x").wait()

    save("x")
    reuse("xq", "qkv", "lse", "ctx", "cq")

    def quant_in(i, _):
        at = pl.ds(pl.multiple_of(i * ROWS, ROWS), ROWS)
        x = xin[r, at, :].astype(F32)
        note_peak(0, x, i * ROWS)
        xq_s[at, :] = (m0 * jnp.tanh(x * i0)).astype(BF16)
        return 0

    lax.fori_loop(0, steps, quant_in, 0)
    save("xq")

    for j in range(3):
        cols = pl.ds(j * width, width)
        proj = dot_nn(xq_s[...], w_qkv[:, cols]) + b_qkv[:, cols]
        qkv_s[:, cols] = proj.astype(BF16)
    save("qkv")

    lane = lax.broadcasted_iota(jnp.int32, (seq, PAIR), 1)
    lo = lane < HEAD_DIM
    key_bias = jnp.where(lax.broadcasted_iota(jnp.int32, (seq, PAIR), 0) < length, 0.0, MASKED).astype(BF16)
    one = jnp.ones((), BF16)
    zero = jnp.zeros((), BF16)

    def attend(p, _):
        at = pl.multiple_of(p * PAIR, PAIR)
        q2 = qkv_s[:, pl.ds(at, PAIR)] * jnp.asarray(HEAD_DIM ** -0.5, BF16)
        k2 = qkv_s[:, pl.ds(pl.multiple_of(width + at, PAIR), PAIR)]
        v2 = qkv_s[:, pl.ds(pl.multiple_of(2 * width + at, PAIR), PAIR)]
        q_a, q_b = jnp.where(lo, q2, one), jnp.where(lo, one, q2)
        k_a = jnp.where(lo, k2, jnp.where(lane == HEAD_DIM, key_bias, zero))
        k_b = jnp.where(lo, jnp.where(lane == 0, key_bias, zero), k2)
        s_a = dot_nt(q_a, k_a)
        s_b = dot_nt(q_b, k_b)
        top_a = jnp.max(s_a, -1, keepdims=True)
        e_a = jnp.exp(s_a - top_a).astype(BF16)
        top_b = jnp.max(s_b, -1, keepdims=True)
        o_a = dot_nn(e_a, jnp.where(lo, v2, one))
        e_b = jnp.exp(s_b - top_b).astype(BF16)
        o_b = dot_nn(e_b, jnp.where(lo, one, v2))
        total = pltpu.roll(jnp.where(lo, o_b, o_a), HEAD_DIM, 1)
        ctx_s[:, pl.ds(at, PAIR)] = jnp.where(lo, o_a, o_b) / total
        lse_s[:, pl.ds(at, PAIR)] = jnp.where(lo, top_a, top_b) + jnp.log(total)
        return 0

    lax.fori_loop(0, width // PAIR, attend, 0)
    save("lse")
    save("ctx")

    def quant_ctx(i, _):
        at = pl.ds(pl.multiple_of(i * ROWS, ROWS), ROWS)
        c = ctx_s[at, :]
        note_peak(1, c, i * ROWS)
        cq_s[at, :] = (m1 * jnp.tanh(c * i1)).astype(BF16)
        return 0

    lax.fori_loop(0, steps, quant_ctx, 0)
    save("cq")
    acc[...] = dot_nn(cq_s[...], w_out[...])
    reuse("n1", "rs1", "hq")

    def norm_one(i, _):
        at = pl.ds(pl.multiple_of(i * ROWS, ROWS), ROWS)
        s = xin[r, at, :].astype(F32) + (acc[at, :] + b_out[...])
        center = s - jnp.mean(s, -1, keepdims=True)
        rs = lax.rsqrt(jnp.mean(center * center, -1, keepdims=True) + EPS)
        n = center * rs
        h = n * gain[0:1, :] + shift[0:1, :]
        n1_s[at, :] = n.astype(BF16)
        rs1_s[at, :] = jnp.broadcast_to(rs, (ROWS, 128))
        hid[at, :] = h
        hq_s[at, :] = (m2 * jnp.tanh(h * i2)).astype(BF16)
        note_peak(2, h, i * ROWS)
        return 0

    lax.fori_loop(0, steps, norm_one, 0)
    save("n1")
    save("rs1")
    save("hq")
    reuse("aq", "sl")

    chunks = ff // CHUNK
    mask_all = row_mask(0, seq)

    def up_chunk(c):
        cols = pl.ds(c * CHUNK, CHUNK)
        up_s[c % 2] = dot_nn(hq_s[...], w_up[:, cols]) + b_up[:, cols]

    def act_chunk(c):
        cols = pl.ds(c * CHUNK, CHUNK)
        act, low, slope = activation(up_s[c % 2], m3, i3)
        aq_s[:, cols] = low.astype(BF16)
        sl_s[:, cols] = slope.astype(BF16)
        top = jnp.where(mask_all, jnp.abs(act), 0.0)
        peaks_o[3] = jnp.maximum(peaks_o[3], peak_rows(top))

    def down_chunk(c):
        cols = pl.ds(c * CHUNK, CHUNK)
        part = dot_nn(aq_s[:, cols], w_down[cols, :])
        if c == 0:
            acc[...] = part
        else:
            acc[...] += part

    up_chunk(0)
    for c in range(chunks):
        if c + 1 < chunks:
            up_chunk(c + 1)
        act_chunk(c)
        if c > 0:
            down_chunk(c - 1)
    down_chunk(chunks - 1)
    save("aq")
    save("sl")
    reuse("n2", "rs2")

    def norm_two(i, _):
        at = pl.ds(pl.multiple_of(i * ROWS, ROWS), ROWS)
        s = hid[at, :] + (acc[at, :] + b_down[...])
        center = s - jnp.mean(s, -1, keepdims=True)
        rs = lax.rsqrt(jnp.mean(center * center, -1, keepdims=True) + EPS)
        n = center * rs
        n2_s[at, :] = n.astype(BF16)
        rs2_s[at, :] = jnp.broadcast_to(rs, (ROWS, 128))
        xout[r, at, :] = (n * gain[1:2, :] + shift[1:2, :]).astype(BF16)
        return 0

    lax.fori_loop(0, steps, norm_two, 0)
    save("n2")
    save("rs2")

    @pl.when(jnp.logical_not(last))
    def _():
        hop(r).start()

    @pl.when(last)
    def _():
        for p in range(count - 1):
            mix_part(r, p).start()
        mix_own(r).start()

    @pl.when(r == rows - 1)
    def _():
        for name in order:
            save_copy(name).wait()

        @pl.when(jnp.logical_not(last))
        def _():
            for i in range(row_count):
                hop(i).wait_send()
            for i in range(row_count):
                mix_part(i, 0).wait_recv()

        @pl.when(last)
        def _():
            for i in range(row_count):
                for p in range(count - 1):
                    mix_part(i, p).wait_send()
                mix_own(i).wait()


def bwd_kernel(count, *refs):
    (
        lens, scales, seeds, w_qkv, w_out, w_up, w_down, gain, shift,
        x_i, qkv_i, lse_i, ctx_i, n1_i, rs1_i, sl_i, n2_i, rs2_i,
        dproj_o, dbr_o, dup_o, ddn_o, gtok_o, small_o,
        gin, gout, x_s, qkv_s, lse_s, ctx_s, n1_s, rs1_s, sl_s, n2_s, rs2_s,
        dproj_s, dbr_s, dup_s, ddn_s, dctx_s, acc, dr,
        load_sem, save_sem, in_sem, send_sem, recv_sem, tok_send, tok_recv,
    ) = refs
    r = pl.program_id(0)
    rows = pl.num_programs(0)
    row_count = seeds.shape[0]
    seq, width = seeds.shape[1], seeds.shape[2]
    ff = w_up.shape[1]
    piece = seq // count
    stage = lax.axis_index("pipe")
    first = stage == 0
    last = stage == count - 1
    steps = seq // ROWS

    loaded = {
        "n2": (n2_i, n2_s), "rs2": (rs2_i, rs2_s), "sl": (sl_i, sl_s), "n1": (n1_i, n1_s),
        "rs1": (rs1_i, rs1_s), "ctx": (ctx_i, ctx_s), "qkv": (qkv_i, qkv_s), "lse": (lse_i, lse_s),
        "x": (x_i, x_s),
    }
    load_order = list(loaded)
    staged = {
        "ddn": (ddn_s, ddn_o), "dup": (dup_s, dup_o), "dbr": (dbr_s, dbr_o), "dproj": (dproj_s, dproj_o),
    }
    save_order = list(staged)

    def load_copy(name, i):
        src, dst = loaded[name]
        return pltpu.make_async_copy(src.at[i], dst, load_sem.at[load_order.index(name)])

    def fetch_next(*names):
        @pl.when(r + 1 < rows)
        def _():
            for name in names:
                load_copy(name, r + 1).start()

    def ready(*names):
        for name in names:
            load_copy(name, r).wait()

    def save_copy(name):
        src, dst = staged[name]
        return pltpu.make_async_copy(src, dst.at[r], save_sem.at[save_order.index(name)])

    def save(name):
        save_copy(name).start()

    def reuse(*names):
        @pl.when(r > 0)
        def _():
            for name in names:
                save_copy(name).wait()

    def seed_copy(i):
        return pltpu.make_async_copy(seeds.at[i], gin.at[i], in_sem.at[i])

    def hop(i):
        return pltpu.make_async_remote_copy(
            src_ref=gout.at[i], dst_ref=gin.at[i], send_sem=send_sem.at[i], recv_sem=recv_sem.at[i],
            device_id={"pipe": lax.rem(stage + count - 1, count)}, device_id_type=LOGICAL,
        )

    def tok_part(i, p):
        return pltpu.make_async_remote_copy(
            src_ref=gout.at[i, pl.ds(p * piece, piece)], dst_ref=gtok_o.at[i],
            send_sem=tok_send.at[i, p], recv_sem=tok_recv.at[i],
            device_id={"pipe": jnp.int32(p)}, device_id_type=LOGICAL,
        )

    def tok_own(i):
        return pltpu.make_async_copy(gout.at[i, pl.ds(0, piece)], gtok_o.at[i], tok_send.at[i, 0])

    @pl.when(r == 0)
    def _():
        greet(stage, count)
        small_o[...] = jnp.zeros_like(small_o)
        for name in load_order:
            load_copy(name, 0).start()

        @pl.when(last)
        def _():
            for i in range(row_count):
                seed_copy(i).start()

    @pl.when(last)
    def _():
        seed_copy(r).wait()

    @pl.when(jnp.logical_not(last))
    def _():
        hop(r).wait_recv()

    length = lens[r]
    m0, m1, m2 = scales[0, 0], scales[0, 1], scales[0, 2]
    i0, i1, i2 = 1.0 / m0, 1.0 / m1, 1.0 / m2

    offsets = {}
    at_col = 0
    for name, size in (
        ("gain0", width), ("gain1", width), ("shift0", width), ("shift1", width),
        ("out", width), ("down", width), ("up", ff), ("qkv", 3 * width),
    ):
        offsets[name] = at_col
        at_col += size

    def add_small(name, v, col=0):
        at = pl.ds(offsets[name] + col, v.shape[1])
        small_o[:, at] += fold_rows(v)

    ready("n2", "rs2")
    reuse("ddn")

    def norm_two(i, _):
        start = pl.multiple_of(i * ROWS, ROWS)
        at = pl.ds(start, ROWS)
        valid = (start + lax.broadcasted_iota(jnp.int32, (ROWS, 1), 0)) < length
        dy = jnp.where(valid, gin[r, at, :].astype(F32), 0.0)
        n = n2_s[at, :].astype(F32)
        rs = rs2_s[at, 0:1]
        dyn = dy * n
        e = dy * gain[1:2, :]
        mean_e = jnp.mean(e, -1, keepdims=True)
        mean_en = jnp.mean(e * n, -1, keepdims=True)
        d = (e - mean_e - n * mean_en) * rs
        dr[at, :] = d
        ddn_s[at, :] = d.astype(BF16)
        add_small("gain1", dyn)
        add_small("shift1", dy)
        add_small("down", d)
        return 0

    lax.fori_loop(0, steps, norm_two, 0)
    save("ddn")
    fetch_next("n2", "rs2")
    ready("sl")
    reuse("dup")

    chunks = ff // CHUNK

    def dact_chunk(c):
        cols = pl.ds(c * CHUNK, CHUNK)
        d = dot_nt(ddn_s[...], w_down[cols, :]) * sl_s[:, cols].astype(F32)
        dup_s[:, cols] = d.astype(BF16)
        add_small("up", d, c * CHUNK)

    def dhid_chunk(c):
        cols = pl.ds(c * CHUNK, CHUNK)
        part = dot_nt(dup_s[:, cols], w_up[:, cols])
        if c == 0:
            acc[...] = part
        else:
            acc[...] += part

    dact_chunk(0)
    for c in range(1, chunks):
        dact_chunk(c)
        dhid_chunk(c - 1)
    dhid_chunk(chunks - 1)
    save("dup")
    fetch_next("sl")
    ready("n1", "rs1")
    reuse("dbr")

    def norm_one(i, _):
        start = pl.multiple_of(i * ROWS, ROWS)
        at = pl.ds(start, ROWS)
        n = n1_s[at, :].astype(F32)
        rs = rs1_s[at, 0:1]
        t = jnp.tanh((n * gain[0:1, :] + shift[0:1, :]) * i2)
        dy = dr[at, :] + acc[at, :] * (1.0 - t * t)
        dyn = dy * n
        e = dy * gain[0:1, :]
        mean_e = jnp.mean(e, -1, keepdims=True)
        mean_en = jnp.mean(e * n, -1, keepdims=True)
        d = (e - mean_e - n * mean_en) * rs
        dr[at, :] = d
        dbr_s[at, :] = d.astype(BF16)
        add_small("gain0", dyn)
        add_small("shift0", dy)
        add_small("out", d)
        return 0

    lax.fori_loop(0, steps, norm_one, 0)
    save("dbr")
    fetch_next("n1", "rs1")
    ready("ctx")
    acc[...] = dot_nt(dbr_s[...], w_out[...])

    def quant_ctx(i, _):
        at = pl.ds(pl.multiple_of(i * ROWS, ROWS), ROWS)
        t = jnp.tanh(ctx_s[at, :] * i1)
        dctx_s[at, :] = (acc[at, :] * (1.0 - t * t)).astype(BF16)
        return 0

    lax.fori_loop(0, steps, quant_ctx, 0)
    ready("qkv", "lse")
    reuse("dproj")

    lane = lax.broadcasted_iota(jnp.int32, (seq, PAIR), 1)
    lo = lane < HEAD_DIM
    spot = jnp.where(lo, lane, lane - HEAD_DIM)
    key_bias = jnp.where(lax.broadcasted_iota(jnp.int32, (seq, PAIR), 0) < length, 0.0, MASKED).astype(BF16)
    one = jnp.ones((), BF16)
    zero = jnp.zeros((), BF16)
    scale = jnp.asarray(HEAD_DIM ** -0.5, BF16)
    src = lax.broadcasted_iota(jnp.int32, (PAIR, PAIR), 0) < HEAD_DIM
    dst = lax.broadcasted_iota(jnp.int32, (PAIR, PAIR), 1) < HEAD_DIM
    swap_sum = jnp.where(src == dst, 0.0, 1.0).astype(BF16)

    def attend(p, _):
        at = pl.multiple_of(p * PAIR, PAIR)
        here = pl.ds(at, PAIR)
        q2 = qkv_s[:, here] * scale
        k2 = qkv_s[:, pl.ds(pl.multiple_of(width + at, PAIR), PAIR)]
        v2 = qkv_s[:, pl.ds(pl.multiple_of(2 * width + at, PAIR), PAIR)]
        do2 = dctx_s[:, here]
        l_hi, l_mid, l_low = split3(pltpu.roll(lse_s[:, here], HEAD_DIM, 1))
        extra_q = jnp.where(
            spot == 0, one, jnp.where(spot == 1, -l_hi, jnp.where(spot == 2, -l_mid, -l_low))
        )
        extra_k = jnp.where(spot == 0, key_bias, jnp.where(spot <= 3, one, zero))
        e_hi, e_mid, e_low = split3(do2.astype(F32) * ctx_s[:, here])
        inner = dot_nn(e_hi, swap_sum) + dot_nn(e_mid, swap_sum)
        d_hi, d_mid, d_low = split3(inner)
        extra_do = jnp.where(spot == 0, -d_hi, jnp.where(spot == 1, -d_mid, -d_low))
        extra_v = jnp.where(spot <= 2, one, zero)
        k_t = k2.T

        def head(is_a):
            mine = lo if is_a else jnp.logical_not(lo)
            s = dot_nt(jnp.where(mine, k2, extra_k), jnp.where(mine, q2, extra_q))
            prob = jnp.exp(s)
            grad_p = dot_nt(jnp.where(mine, v2, extra_v), jnp.where(mine, do2, extra_do))
            grad_v = dot_nn(prob.astype(BF16), do2)
            grad_s = (prob * grad_p).astype(BF16)
            grad_k = dot_nn(grad_s, q2)
            half = k_t[0:HEAD_DIM] if is_a else k_t[HEAD_DIM:PAIR]
            return dot_nn(half, grad_s), grad_k, grad_v

        qa, ka, va = head(True)
        qb, kb, vb = head(False)
        grad_q = jnp.concatenate([qa, qb], 0).T * (HEAD_DIM ** -0.5)
        dproj_s[:, here] = grad_q.astype(BF16)
        dproj_s[:, pl.ds(pl.multiple_of(width + at, PAIR), PAIR)] = jnp.where(lo, ka, kb).astype(BF16)
        dproj_s[:, pl.ds(pl.multiple_of(2 * width + at, PAIR), PAIR)] = jnp.where(lo, va, vb).astype(BF16)
        return 0

    lax.fori_loop(0, width // PAIR, attend, 0)
    save("dproj")
    fetch_next("ctx", "qkv", "lse")
    for j in range(3):
        cols = pl.ds(j * width, width)
        part = dot_nt(dproj_s[:, cols], w_qkv[:, cols])
        if j == 0:
            acc[...] = part
        else:
            acc[...] += part
        if j != 1:
            add_small("qkv", dproj_s[:, cols].astype(F32), j * width)
    ready("x")

    def quant_in(i, _):
        at = pl.ds(pl.multiple_of(i * ROWS, ROWS), ROWS)
        t = jnp.tanh(x_s[at, :].astype(F32) * i0)
        gout[r, at, :] = (dr[at, :] + acc[at, :] * (1.0 - t * t)).astype(BF16)
        return 0

    lax.fori_loop(0, steps, quant_in, 0)
    fetch_next("x")

    @pl.when(jnp.logical_not(first))
    def _():
        hop(r).start()

    @pl.when(first)
    def _():
        for p in range(1, count):
            tok_part(r, p).start()
        tok_own(r).start()

    @pl.when(r == rows - 1)
    def _():
        for name in save_order:
            save_copy(name).wait()

        @pl.when(jnp.logical_not(first))
        def _():
            for i in range(row_count):
                hop(i).wait_send()
            for i in range(row_count):
                tok_part(i, 0).wait_recv()

        @pl.when(first)
        def _():
            for i in range(row_count):
                for p in range(1, count):
                    tok_part(i, p).wait_send()
                tok_own(i).wait()


def whole(a):
    return pl.BlockSpec(a.shape, lambda r, n=a.ndim: (0,) * n, pipeline_mode=pl.Buffered(1))


ANYWHERE = pl.BlockSpec(memory_space=pl.ANY)
SCALAR = pl.BlockSpec(memory_space=pltpu.SMEM)
VMEM_LIMIT = 60 * 1024 * 1024


def run_forward(count, tokens, lengths, scales, weights):
    w_qkv, b_qkv, w_out, b_out, w_up, b_up, w_down, b_down, gain, shift = weights
    rows, seq, width = tokens.shape
    ff = w_up.shape[1]
    big = lambda n, t: jax.ShapeDtypeStruct((rows, seq, n), t)
    saves = [
        (width, BF16), (width, BF16), (3 * width, BF16), (width, F32), (width, F32), (width, BF16),
        (width, BF16), (128, F32), (width, BF16), (ff, BF16), (ff, BF16), (width, BF16), (128, F32),
    ]
    dense = (w_qkv, b_qkv, w_out, b_out, w_up, b_up, w_down, b_down, gain, shift)
    tok = rows * seq
    return pl.pallas_call(
        lambda *refs: fwd_kernel(count, *refs),
        grid=(rows,),
        in_specs=[SCALAR, SCALAR, ANYWHERE] + [whole(a) for a in dense],
        out_specs=[ANYWHERE] * 14 + [pl.BlockSpec((4, 8, 128), lambda r: (0, 0, 0))],
        out_shape=[big(n, t) for n, t in saves]
        + [
            jax.ShapeDtypeStruct((rows, seq // count, width), BF16),
            jax.ShapeDtypeStruct((4, 8, 128), F32),
        ],
        scratch_shapes=[pltpu.VMEM((rows, seq, width), BF16), pltpu.VMEM((rows, seq, width), BF16)]
        + [pltpu.VMEM((seq, n), t) for n, t in saves[1:]]
        + [
            pltpu.VMEM((seq, width), F32),
            pltpu.VMEM((seq, width), F32),
            pltpu.VMEM((2, seq, CHUNK), F32),
            pltpu.SemaphoreType.DMA((13,)),
            pltpu.SemaphoreType.DMA((rows,)),
            pltpu.SemaphoreType.DMA((rows,)),
            pltpu.SemaphoreType.DMA((rows,)),
            pltpu.SemaphoreType.DMA((rows, count)),
            pltpu.SemaphoreType.DMA((rows,)),
        ],
        compiler_params=pltpu.CompilerParams(
            collective_id=0, has_side_effects=True, vmem_limit_bytes=VMEM_LIMIT,
            dimension_semantics=("arbitrary",),
        ),
        cost_estimate=pl.CostEstimate(
            flops=2 * tok * (4 * width * width + 2 * width * ff + 2 * seq * width),
            bytes_accessed=tok * 28000, transcendentals=tok * 3 * ff,
        ),
    )(lengths, scales, tokens, *dense)


def run_backward(count, seeds, lengths, scales, weights, kept):
    w_qkv, b_qkv, w_out, b_out, w_up, b_up, w_down, b_down, gain, shift = weights
    x, xq, qkv, lse, ctx, cq, n1, rs1, hq, aq, sl, n2, rs2 = kept
    rows, seq, width = seeds.shape
    ff = w_up.shape[1]
    big = lambda n, t: jax.ShapeDtypeStruct((rows, seq, n), t)
    saves = [(3 * width, BF16), (width, BF16), (ff, BF16), (width, BF16)]
    loads = (x, qkv, lse, ctx, n1, rs1, sl, n2, rs2)
    dense = (w_qkv, w_out, w_up, w_down, gain, shift)
    tok = rows * seq
    small = 6 * width + ff + 3 * width
    return pl.pallas_call(
        lambda *refs: bwd_kernel(count, *refs),
        grid=(rows,),
        in_specs=[SCALAR, SCALAR, ANYWHERE] + [whole(a) for a in dense] + [ANYWHERE] * 9,
        out_specs=[ANYWHERE] * 5 + [pl.BlockSpec((8, small), lambda r: (0, 0))],
        out_shape=[big(n, t) for n, t in saves]
        + [
            jax.ShapeDtypeStruct((rows, seq // count, width), BF16),
            jax.ShapeDtypeStruct((8, small), F32),
        ],
        scratch_shapes=[pltpu.VMEM((rows, seq, width), BF16), pltpu.VMEM((rows, seq, width), BF16)]
        + [pltpu.VMEM(a.shape[1:], a.dtype) for a in loads]
        + [pltpu.VMEM((seq, n), t) for n, t in saves]
        + [
            pltpu.VMEM((seq, width), BF16),
            pltpu.VMEM((seq, width), F32),
            pltpu.VMEM((seq, width), F32),
            pltpu.SemaphoreType.DMA((9,)),
            pltpu.SemaphoreType.DMA((4,)),
            pltpu.SemaphoreType.DMA((rows,)),
            pltpu.SemaphoreType.DMA((rows,)),
            pltpu.SemaphoreType.DMA((rows,)),
            pltpu.SemaphoreType.DMA((rows, count)),
            pltpu.SemaphoreType.DMA((rows,)),
        ],
        compiler_params=pltpu.CompilerParams(
            collective_id=1, has_side_effects=True, vmem_limit_bytes=VMEM_LIMIT,
            dimension_semantics=("arbitrary",),
        ),
        cost_estimate=pl.CostEstimate(
            flops=2 * tok * (4 * width * width + 2 * width * ff + 5 * seq * width),
            bytes_accessed=tok * 28000, transcendentals=tok * ff,
        ),
    )(lengths, scales, seeds, *dense, *loads)


def weight_grad(left, right):
    g = jnp.einsum("rsd,rse->de", left, right, preferred_element_type=F32).astype(BF16)
    return lax.psum_scatter(g, "dp", scatter_dimension=0, tiled=True).astype(F32)


def max_over(v, axis):
    size = lax.axis_size(axis)
    shift = 1
    while shift < size:
        v = jnp.maximum(v, lax.ppermute(v, axis, [(i, (i + shift) % size) for i in range(size)]))
        shift *= 2
    return v


def shards(
    tokens, lengths, ema_scales, w_qkv, bias_qv, w_out, bias_out, w_up, bias_up, w_down, bias_down,
    ln_gain, ln_bias, cotangent,
):
    count = lax.axis_size("pipe")
    width = tokens.shape[2]
    ff = w_up.shape[2]
    b_qkv = jnp.concatenate([bias_qv[:, :width], jnp.zeros_like(bias_qv[:, :width]), bias_qv[:, width:]], 1)
    weights = (
        w_qkv[0], b_qkv, w_out[0], bias_out, w_up[0], bias_up, w_down[0], bias_down, ln_gain[0], ln_bias[0],
    )
    *kept, mixed, peaks = run_forward(count, tokens, lengths, ema_scales, weights)
    x, xq, qkv, lse, ctx, cq, n1, rs1, hq, aq, sl, n2, rs2 = kept
    dproj, dbr, dup, ddn, grad_tokens, small = run_backward(
        count, cotangent, lengths, ema_scales, weights, kept
    )
    batch_max = max_over(jnp.max(peaks, (1, 2))[None], "dp")
    g_down = weight_grad(aq, ddn)
    g_up = weight_grad(hq, dup)
    g_out = weight_grad(cq, dbr)
    g_qkv = weight_grad(xq, dproj)
    n = lax.axis_size("dp")
    sums = jnp.sum(small, 0)
    parts, at = [], 0
    for size in (width, width, width, width, width, width, ff, 3 * width):
        parts.append(sums[at : at + size])
        at += size
    gain0, gain1, shift0, shift1, s_out, s_down, s_up, s_qkv = parts
    s_qv = jnp.concatenate([s_qkv[:width], s_qkv[2 * width :]])
    packed = jnp.concatenate(
        [v.reshape(n, -1) for v in (gain0, gain1, shift0, shift1, s_out, s_down, s_up, s_qv)], 1
    )
    mine = lax.psum_scatter(packed, "dp", scatter_dimension=0, tiled=True)
    outs, at = [], 0
    for size in (width, width, width, width, width, width, ff, 2 * width):
        outs.append(mine[:, at : at + size // n])
        at += size // n
    gain0, gain1, shift0, shift1, s_out, s_down, s_up, s_qv = outs
    g_gain = jnp.stack([gain0, gain1], 1)
    g_shift = jnp.stack([shift0, shift1], 1)
    return (
        mixed, grad_tokens, g_qkv[None], s_qv, g_out[None], s_out, g_up[None], s_up, g_down[None], s_down,
        g_gain, g_shift, batch_max,
    )


def solution(mesh):
    return jax.shard_map(
        shards,
        mesh=mesh,
        in_specs=(
            P("dp", None, None), P("dp"), P("pipe", None), P("pipe", None, None), P("pipe", None),
            P("pipe", None, None), P("pipe", None), P("pipe", None, None), P("pipe", None),
            P("pipe", None, None), P("pipe", None), P("pipe", None, None), P("pipe", None, None),
            P("dp", None, None),
        ),
        out_specs=(
            P("dp", "pipe", None), P("dp", "pipe", None), P("pipe", "dp", None), P("pipe", "dp"),
            P("pipe", "dp", None), P("pipe", "dp"), P("pipe", "dp", None), P("pipe", "dp"),
            P("pipe", "dp", None), P("pipe", "dp"), P("pipe", None, "dp"), P("pipe", None, "dp"),
            P("pipe", None),
        ),
        check_vma=False,
    )
```

time: 2200 us -> 780 us (0.35)
  matrix products: 891 us -> 48.3 us
  other arithmetic: 450 us -> 9.87 us
  local copies, waits for them, and re-layouts: 426 us -> 11.9 us
  Pallas kernels: 0 us -> 399 us
  waiting for transfers between devices: 313 us -> 247 us
  starting transfers between devices: 28 us -> 1.75 us
    dot_general x133 -> x4, matrix products: 891 us -> 48.3 us  [weight_grad(): jnp.einsum('rsd,rse->de', left, right, preferred_element_type=F32)]
    pallas_call x0 -> x2, Pallas kernels: none -> 399 us  [the longest x1 207 us: run_forward(): pl.pallas_call(lambda *refs: fwd_kernel(count, *refs), grid=(rows,), in_s...]
    dynamic_update_slice x82 -> x0, other arithmetic: 236 us -> none  [the longest x75 218 us: place_one(): lax.dynamic_update_index_in_dim(whole_buf, jnp.where(active_tick, new_pie...]
    dynamic_slice x84 -> x0, local copies, waits for them, and re-layouts: 203 us -> none  [the longest x60 139 us: place_one(): lax.dynamic_index_in_dim(whole_buf, slot_index, 0, keepdims=False)]
    reduce_sum x67 -> x1, other arithmetic: 74.3 us -> 0.08 us  [shards(): sums = jnp.sum(small, 0)]
    reduce_scatter x6 -> x4, waiting for transfers between devices: 298 us -> 237 us  [weight_grad(): lax.psum_scatter(g, 'dp', scatter_dimension=0, tiled=True).astype(F32)]
    convert_element_type x13 -> x0, other arithmetic: 58.7 us -> none  [the longest x7 51.5 us: attend_back(): (probabilities * (grad_probs - row_inner)).astype(jnp.bfloat16)]
    unnamed x1211 -> x19, local copies, waits for them, and re-layouts: 56.6 us -> 6.71 us
  transfers between devices with their start and end apart: 20 -> 7, of which waited for: 6 -> 5; matrix products, arithmetic and copies ran while one was open for 34% -> 7% of each run, Pallas kernels for 0% -> 0%
where the time goes in v1:
time: 780 us; the launch traced here: 769 us
  Pallas kernels  399 us (51%)
  waiting for transfers between devices  247 us (32%)
  matrix products  48.3 us (6%)
  blocking collectives  37 us (5%)
  between operations  14.3 us (2%)
  local copies, waits for them, and re-layouts  11.9 us (2%)
  other arithmetic  9.87 us (1%)
    reduce_scatter x4, waiting for transfers between devices, weight_grad(): lax.psum_scatter(g, 'dp', scatter_dimension=0, tiled=True).astype(F32)  237 us
    pallas_call x1, Pallas kernels, run_forward(): pl.pallas_call(lambda *refs: fwd_kernel(count, *refs), grid=(rows,), in_s...  207 us
    pallas_call x1, Pallas kernels, run_backward(): pl.pallas_call(lambda *refs: bwd_kernel(count, *refs), grid=(rows,), in_s...  192 us
    dot_general x4, matrix products, weight_grad(): jnp.einsum('rsd,rse->de', left, right, preferred_element_type=F32)  48.3 us
    unnamed x1, blocking collectives  37 us
  transfers between devices with their start and end apart: 7, of which 5 were waited for; matrix products, arithmetic and copies ran while one was open for 7% of the time, Pallas kernels for 0%

profile of v1, /device:TPU:0, one launch (start us, length us, event | category | flops | bytes accessed | tf_op | source)
XLA Modules:
  0.0 769.3 jit_solution(5554895195199206851)
XLA Ops:
  7.2 0.0 reduce-scatter.7.cloned.1.call-start
  7.2 0.7 fusion.2
  7.9 0.6 fusion.refs_4_
  8.6 206.9 %shard_map.237 = (bf16[4,512,768]{2,1,0:T(8,128)(2,1)}, bf16[4,512,768]{2,1,0:T(8,128)(2,1)}, bf16[4,512,2304]{2,1,0:T(8,128)(2,1)}, f32[4,512,768]{2,1,0:T(8,12...) custom-call(s32[4]{0:T(128)} %refs_0_.3, ...), custom_call_target="tpu_custom_call" | custom-call | flops 32212254720 | bytes 57344000 | tf_op jit(solution)/shard_map/pallas_call | solution.py:662
  215.5 0.0 copy-start.5
  215.5 192.1 %shard_map.238 = (bf16[4,512,2304]{2,1,0:T(8,128)(2,1)}, bf16[4,512,768]{2,1,0:T(8,128)(2,1)}, bf16[4,512,3072]{2,1,0:T(8,128)(2,1)}, bf16[4,512,768]{2,1,0:T(8,...) custom-call(s32[4]{0:T(128)} %refs_0_.3, f32[1,4]{1,0:T(1,128)} %refs_1_.3, bf16[4,512,768]{2,1,0:T(8,128)(2,1)} %refs_2_.3, ...), custom_call_target="tpu_custom_call" | custom-call | flops 37044092928 | bytes 57344000 | tf_op jit(solution)/shard_map/pallas_call | solution.py:707
  407.6 0.0 copy-done.5
  407.6 5.6 bitcast_convert_fusion.3
  413.2 0.0 reduce-scatter.7.cloned.1.call-update
  413.2 0.0 reduce-scatter.5.cloned.1.call-start
  413.2 13.4 %bitcast_convert_fusion.2 = bf16[768,2304]{1,0:T(8,128)(2,1)} fusion(bf16[4,512,768]{2,1,0:T(8,128)(2,1)} %get-tuple-element.45, bf16[4,512,2304]{2,1,0:T(8,128)(2,1)} %get-tuple-element.46), kind=kOutput, calls=%fused_computation.2 | convolution fusion | flops 7249526784 | bytes 16121856 | tf_op jit(solution)/shard_map/rsd,rse->de/dot_general | solution.py:744
  426.6 0.0 copy-start.7
  426.6 0.0 reduce-scatter.5.cloned.1.call-update
  426.7 0.0 reduce-scatter.11.cloned.1.call-start
  426.7 1.8 copy-done.7
  428.5 14.6 %bitcast_convert_fusion = bf16[3072,768]{1,0:T(8,128)(2,1)} fusion(bf16[4,512,3072]{2,1,0:T(8,128)(2,1)} %get-tuple-element.52, bf16[4,512,768]{2,1,0:T(8,128)(2,1)S(1)} %copy-done.7), kind=kOutput, calls=%fused_computation | convolution fusion | flops 9666035712 | bytes 20447232 | tf_op jit(solution)/shard_map/rsd,rse->de/dot_general | solution.py:744
  443.1 0.0 reduce-scatter.11.cloned.1.call-update
  443.1 0.0 reduce-scatter.9.cloned.1.call-start
  443.2 1.8 copy-done.6
  445.0 14.7 %bitcast_convert_fusion.1 = bf16[768,3072]{1,0:T(8,128)(2,1)} fusion(bf16[4,512,768]{2,1,0:T(8,128)(2,1)S(1)} %copy-done.6, bf16[4,512,3072]{2,1,0:T(8,128)(2,1)} %get-tuple-element.51), kind=kOutput, calls=%fused_computation.1 | convolution fusion | flops 9666035712 | bytes 20447232 | tf_op jit(solution)/shard_map/rsd,rse->de/dot_general | solution.py:744
  459.8 0.0 copy-start.3
  459.8 0.0 copy-start.2
  459.8 0.0 copy-start.4
  459.8 0.0 reduce-scatter.9.cloned.1.call-update
  459.8 0.0 copy-start
  459.8 0.7 copy-done.3
  460.5 0.1 reduce_max.9
  460.6 1.5 collective-permute-start
  462.1 0.0 copy-done.2
  462.1 0.1 reduce_sum.9
  462.2 0.1 concatenate.15
  462.3 0.1 concatenate.16
  462.4 0.1 reshape.118
  462.5 0.1 reshape.119
  462.5 0.1 reshape.120
  462.6 0.1 reshape.121
  462.7 0.1 reshape.122
  462.8 0.1 reshape.123
  462.8 0.0 copy-done.4
  462.8 0.6 dynamic-slice
  463.4 0.1 concatenate.18
  463.5 37.0 %all-reduce = f32[8,1152]{1,0:T(8,128)S(1)} all-reduce(f32[8,1152]{1,0:T(8,128)S(1)} %concatenate.18), channel_id=3, replica_groups=mesh['dp'=8,'pipe'=4] {'dp'}, use_global_device_ids=true, to_apply=%region_2.0.clone | all-reduce | flops 9216 | bytes 73728
  500.5 1.3 dynamic-slice.4
  501.8 1.3 dynamic-slice.2
  503.1 1.2 dynamic-slice_bitcast_fusion.1
  504.3 0.6 pad_maximum_fusion.1
  504.9 0.0 collective-permute-done
  504.9 0.1 collective-permute-start.1
  505.0 5.3 collective-permute-done.1
  510.3 0.0 collective-permute-start.2
  510.3 4.5 collective-permute-done.2
  514.8 0.5 max.11
  515.4 0.0 reduce-scatter.7.cloned.1.call-done
  515.4 1.6 bitcast_convert_fusion.7
  517.0 44.2 %reduce-scatter.5.cloned.1.call-done = bf16[96,2304]{1,0:T(8,128)(2,1)} async-done(((bf16[768,2304]{1,0:T(8,128)(2,1)}), bf16[96,2304]{1,0:T(8,128)(2,1)}) %reduce-scatter.5.cloned.1.call-update) | async-done | bytes 442384 | tf_op jit(solution)/shard_map/reduce_scatter | solution.py:745
  561.2 2.0 bitcast_convert_fusion.6
  563.2 96.7 %reduce-scatter.11.cloned.1.call-done = bf16[384,768]{1,0:T(8,128)(2,1)} async-done(((bf16[3072,768]{1,0:T(8,128)(2,1)}), bf16[384,768]{1,0:T(8,128)(2,1)}) %reduce-scatter.11.cloned.1.call-update) | async-done | bytes 589840 | tf_op jit(solution)/shard_map/reduce_scatter | solution.py:745
  659.8 2.2 bitcast_convert_fusion.4
  662.0 96.4 %reduce-scatter.9.cloned.1.call-done = bf16[96,3072]{1,0:T(8,128)(2,1)} async-done(((bf16[768,3072]{1,0:T(8,128)(2,1)}), bf16[96,3072]{1,0:T(8,128)(2,1)}) %reduce-scatter.9.cloned.1.call-update) | async-done | bytes 589840 | tf_op jit(solution)/shard_map/reduce_scatter | solution.py:745
  758.4 2.2 bitcast_convert_fusion.5
  760.5 0.0 copy-done
  760.5 0.9 copy.41
  761.4 0.0 copy-done.1
  761.4 0.9 copy.42
  (10 shorter events, 0.0 us)
Async XLA Ops:
  7.2 508.2 %reduce-scatter.7.cloned.1.call-start = ((), (), s32[]{:S(2)}) async-start(), calls=%async_computation.5 | async-start | bytes 1327104 | tf_op jit(solution)/shard_map/reduce_scatter | solution.py:745
  215.5 192.1 %copy-start.5 = (bf16[4,512,768]{2,1,0:T(8,128)(2,1)S(1)}, bf16[4,512,768]{2,1,0:T(8,128)(2,1)}, u32[]{:S(2)}) copy-start(bf16[4,512,768]{2,1,0:T(8,128)(2,1)} %get-tuple-element.48) | copy-start | bytes 9437188
  413.2 148.0 %reduce-scatter.5.cloned.1.call-start = ((), (), s32[]{:S(2)}) async-start(), calls=%async_computation.4 | async-start | bytes 3981312 | tf_op jit(solution)/shard_map/reduce_scatter | solution.py:745
  426.6 1.9 copy-start.7
  426.7 233.2 %reduce-scatter.11.cloned.1.call-start = ((), (), s32[]{:S(2)}) async-start(), calls=%async_computation.7 | async-start | bytes 5308416 | tf_op jit(solution)/shard_map/reduce_scatter | solution.py:745
  443.1 1.9 copy-start.6
  443.1 315.2 %reduce-scatter.9.cloned.1.call-start = ((), (), s32[]{:S(2)}) async-start(), calls=%async_computation.6 | async-start | bytes 5308416 | tf_op jit(solution)/shard_map/reduce_scatter | solution.py:745
  459.8 0.7 copy-start.3
  459.8 2.4 copy-start.2
  459.8 3.1 copy-start.4
  459.8 300.8 %copy-start = (bf16[4,128,768]{2,1,0:T(8,128)(2,1)S(1)}, bf16[4,128,768]{2,1,0:T(8,128)(2,1)}, u32[]{:S(2)}) copy-start(bf16[4,128,768]{2,1,0:T(8,128)(2,1)} %get-tuple-element.86) | copy-start | bytes 2359300
  460.6 44.3 %collective-permute-start = (f32[1,4]{1,0:T(1,128)S(1)}, f32[1,4]{1,0:T(1,128)S(1)}, u32[]{:S(2)}, u32[]{:S(2)}) collective-permute-start(f32[1,4]{1,0:T(1,128)S(1)} %bitcast.45), channel_id=1, source_target_pairs={{0,4},{4,8},{8,12},{12,16},{16,20},{20,24},{24,28},{28,0},{1,5},{5... | collective-permute-start | bytes 56 | tf_op jit(solution)/shard_map/ppermute | solution.py:752
  504.9 5.4 collective-permute-start.1
  510.3 4.5 collective-permute-start.2
  517.0 244.4 %copy-start.1 = (bf16[4,128,768]{2,1,0:T(8,128)(2,1)S(1)}, bf16[4,128,768]{2,1,0:T(8,128)(2,1)}, u32[]{:S(2)}) copy-start(bf16[4,128,768]{2,1,0:T(8,128)(2,1)} %get-tuple-element.87) | copy-start | bytes 2359300
Sparse Core Ops, SparseCore 0:
  413.3 65.9 reduce-scatter.6
  482.9 78.2 reduce-scatter.4
  564.8 94.9 reduce-scatter.10
  663.3 94.9 reduce-scatter.8

commit v2 on v1

--- a/solution.py
+++ b/solution.py
@@ -34,6 +34,10 @@
 
 def dot_nt(a, b):
     return lax.dot_general(a, b, (((1,), (1,)), ((), ())), preferred_element_type=F32)
+
+
+def dot_tn(a, b):
+    return lax.dot_general(a, b, (((0,), (0,)), ((), ())), preferred_element_type=F32)
 
 
 def fold_rows(v):
@@ -341,7 +345,7 @@
         dproj_o, dbr_o, dup_o, ddn_o, gtok_o, small_o,
         gin, gout, x_s, qkv_s, lse_s, ctx_s, n1_s, rs1_s, sl_s, n2_s, rs2_s,
         dproj_s, dbr_s, dup_s, ddn_s, dctx_s, acc, dr,
-        load_sem, save_sem, in_sem, send_sem, recv_sem, tok_send, tok_recv,
+        load_sem, save_sem, in_sem, send_sem, recv_sem, tok_send,
     ) = refs
     r = pl.program_id(0)
     rows = pl.num_programs(0)
@@ -401,15 +405,8 @@
             device_id={"pipe": lax.rem(stage + count - 1, count)}, device_id_type=LOGICAL,
         )
 
-    def tok_part(i, p):
-        return pltpu.make_async_remote_copy(
-            src_ref=gout.at[i, pl.ds(p * piece, piece)], dst_ref=gtok_o.at[i],
-            send_sem=tok_send.at[i, p], recv_sem=tok_recv.at[i],
-            device_id={"pipe": jnp.int32(p)}, device_id_type=LOGICAL,
-        )
-
-    def tok_own(i):
-        return pltpu.make_async_copy(gout.at[i, pl.ds(0, piece)], gtok_o.at[i], tok_send.at[i, 0])
+    def tok_copy(i):
+        return pltpu.make_async_copy(gout.at[i], gtok_o.at[i], tok_send.at[i])
 
     @pl.when(r == 0)
     def _():
@@ -615,9 +612,7 @@
 
     @pl.when(first)
     def _():
-        for p in range(1, count):
-            tok_part(r, p).start()
-        tok_own(r).start()
+        tok_copy(r).start()
 
     @pl.when(r == rows - 1)
     def _():
@@ -628,15 +623,11 @@
         def _():
             for i in range(row_count):
                 hop(i).wait_send()
+
+        @pl.when(first)
+        def _():
             for i in range(row_count):
-                tok_part(i, 0).wait_recv()
-
-        @pl.when(first)
-        def _():
-            for i in range(row_count):
-                for p in range(1, count):
-                    tok_part(i, p).wait_send()
-                tok_own(i).wait()
+                tok_copy(i).wait()
 
 
 def whole(a):
@@ -710,10 +701,7 @@
         in_specs=[SCALAR, SCALAR, ANYWHERE] + [whole(a) for a in dense] + [ANYWHERE] * 9,
         out_specs=[ANYWHERE] * 5 + [pl.BlockSpec((8, small), lambda r: (0, 0))],
         out_shape=[big(n, t) for n, t in saves]
-        + [
-            jax.ShapeDtypeStruct((rows, seq // count, width), BF16),
-            jax.ShapeDtypeStruct((8, small), F32),
-        ],
+        + [big(width, BF16), jax.ShapeDtypeStruct((8, small), F32)],
         scratch_shapes=[pltpu.VMEM((rows, seq, width), BF16), pltpu.VMEM((rows, seq, width), BF16)]
         + [pltpu.VMEM(a.shape[1:], a.dtype) for a in loads]
         + [pltpu.VMEM((seq, n), t) for n, t in saves]
@@ -726,7 +714,6 @@
             pltpu.SemaphoreType.DMA((rows,)),
             pltpu.SemaphoreType.DMA((rows,)),
             pltpu.SemaphoreType.DMA((rows,)),
-            pltpu.SemaphoreType.DMA((rows, count)),
             pltpu.SemaphoreType.DMA((rows,)),
         ],
         compiler_params=pltpu.CompilerParams(
@@ -740,18 +727,335 @@
     )(lengths, scales, seeds, *dense, *loads)
 
 
+def ring_to_dp(pos, n):
+    return jnp.where(pos < n // 2, 2 * pos, 2 * (n - pos) - 1)
+
+
+def dp_to_ring(j, n):
+    return jnp.where(j % 2 == 0, j // 2, n - 1 - j // 2)
+
+
+def grad_kernel(count, n, *refs):
+    (
+        aq, hq, cq, xq, ddn, dbr, dup, dproj, small, g0,
+        gq_o, go_o, gu_o, gd_o, small_o, gtok_o,
+        slots_d, slots_u, slots_q, slots_s, aq_v, ddn_v, left_v, right_v, own_u, own_q,
+        aq_sem, ddn_sem, left_sem, right_sem,
+        send_d, recv_d, send_u, recv_u, send_q, recv_q, send_s, recv_s, tok_send, tok_recv,
+    ) = refs
+    width = ddn.shape[1]
+    ff = aq.shape[1]
+    shard, shard_ff = width // n, ff // n
+    row_count, seq = g0.shape[0], g0.shape[1]
+    piece = seq // count
+    stage = lax.axis_index("pipe")
+    me = lax.axis_index("dp")
+    pos = dp_to_ring(me, n)
+    first = stage == 0
+    ahead = ring_to_dp(lax.rem(pos + 1, n), n)
+    behind = ring_to_dp(lax.rem(pos + n - 1, n), n)
+    target = (ahead, behind)
+
+    barrier = pltpu.get_barrier_semaphore()
+    for peer in target:
+        pl.semaphore_signal(barrier, inc=1, device_id={"dp": peer}, device_id_type=LOGICAL)
+
+    @pl.when(first)
+    def _():
+        pl.semaphore_wait(barrier, 1 + count)
+
+    @pl.when(jnp.logical_not(first))
+    def _():
+        pl.semaphore_signal(barrier, inc=1, device_id={"pipe": jnp.int32(0)}, device_id_type=LOGICAL)
+        pl.semaphore_wait(barrier, 2)
+
+    def tok_part(i, p):
+        return pltpu.make_async_remote_copy(
+            src_ref=g0.at[i, pl.ds(p * piece, piece)], dst_ref=gtok_o.at[i],
+            send_sem=tok_send.at[i, p], recv_sem=tok_recv.at[i],
+            device_id={"pipe": jnp.int32(p)}, device_id_type=LOGICAL,
+        )
+
+    def tok_own(i):
+        return pltpu.make_async_copy(g0.at[i, pl.ds(0, piece)], gtok_o.at[i], tok_send.at[i, 0])
+
+    def chunk(d, step):
+        at = pos + 2 * n - 1 - step if d == 0 else pos + 1 + step
+        return ring_to_dp(lax.rem(at, n), n)
+
+    def aq_copy(d, step, slot):
+        cols = pl.ds(pl.multiple_of(chunk(d, step) * shard_ff, 128), shard_ff)
+        return pltpu.make_async_copy(aq.at[:, cols], aq_v.at[d, slot], aq_sem.at[d, slot])
+
+    blocks = [(hq, dup, i, own_u, i) for i in range(ff // width)]
+    blocks += [(xq, dproj, i, own_q, i) for i in range(3)] + [(cq, dbr, 0, own_q, 3)]
+    lefts = [hq, xq, cq]
+
+    def left_copy(k):
+        return pltpu.make_async_copy(lefts[k], left_v.at[k % 2], left_sem.at[k])
+
+    def right_copy(b):
+        return pltpu.make_async_copy(
+            blocks[b][1].at[:, pl.ds(blocks[b][2] * width, width)], right_v.at[b % 2], right_sem.at[b]
+        )
+
+    def block_left(b):
+        return [k for k in range(3) if lefts[k] is blocks[b][0]][0]
+
+    ddn_copy = pltpu.make_async_copy(ddn, ddn_v, ddn_sem.at[0])
+    ddn_copy.start()
+    for d in range(2):
+        aq_copy(d, 0, 0).start()
+    left_copy(0).start()
+    right_copy(0).start()
+    right_copy(1).start()
+    left_copy(1).start()
+
+    @pl.when(first)
+    def _():
+        for i in range(row_count):
+            for p in range(1, count):
+                tok_part(i, p).start()
+            tok_own(i).start()
+
+    ddn_copy.wait()
+
+    def product(b):
+        k = block_left(b)
+        if b == 0 or block_left(b - 1) != k:
+            left_copy(k).wait()
+        right_copy(b).wait()
+        part = dot_tn(left_v[k % 2], right_v[b % 2])
+        blocks[b][3][:, pl.ds(blocks[b][4] * width, width)] = part.astype(BF16)
+        if b + 2 < len(blocks):
+            right_copy(b + 2).start()
+        if k + 2 < 3 and block_left(b + 1) != k:
+            left_copy(k + 2).start()
+
+    def lane(slots, send, recv, d, step, own, finish):
+        def message(at):
+            return pltpu.make_async_remote_copy(
+                src_ref=slots.at[d, at], dst_ref=slots.at[d, jnp.minimum(at + 1, n - 1)],
+                send_sem=send.at[d, at], recv_sem=recv.at[d, jnp.minimum(at + 1, n - 1)],
+                device_id={"dp": target[d]}, device_id_type=LOGICAL,
+            )
+
+        def arrived(at):
+            return pltpu.make_async_remote_copy(
+                src_ref=slots.at[d, at], dst_ref=slots.at[d, at],
+                send_sem=send.at[d, at], recv_sem=recv.at[d, at],
+                device_id={"dp": target[d]}, device_id_type=LOGICAL,
+            )
+
+        if own is None:
+            return message
+
+        @pl.when(step == 0)
+        def _():
+            slots[d, 0] = own().astype(BF16)
+
+        @pl.when(step > 0)
+        def _():
+            mine = own()
+            arrived(step).wait_recv()
+            total = slots[d, step].astype(F32) + mine
+
+            @pl.when(step < n - 1)
+            def _():
+                slots[d, step] = total.astype(BF16)
+
+            @pl.when(step == n - 1)
+            def _():
+                finish(total)
+
+        @pl.when(step < n - 1)
+        def _():
+            message(step).start()
+
+    def small_message(at):
+        return pltpu.make_async_remote_copy(
+            src_ref=slots_s.at[at], dst_ref=slots_s.at[jnp.minimum(at + 1, n - 1)],
+            send_sem=send_s.at[at], recv_sem=recv_s.at[jnp.minimum(at + 1, n - 1)],
+            device_id={"dp": target[0]}, device_id_type=LOGICAL,
+        )
+
+    def small_arrived(at):
+        return pltpu.make_async_remote_copy(
+            src_ref=slots_s.at[at], dst_ref=slots_s.at[at], send_sem=send_s.at[at],
+            recv_sem=recv_s.at[at], device_id={"dp": target[0]}, device_id_type=LOGICAL,
+        )
+
+    half = width // 2
+    sum_rows = lax.broadcasted_iota(jnp.int32, (16, 128), 0) < 9
+
+    def small_step(step):
+        mine = small[chunk(0, step)]
+
+        @pl.when(step == 0)
+        def _():
+            slots_s[0] = mine
+
+        @pl.when(step > 0)
+        def _():
+            small_arrived(step).wait_recv()
+            got = slots_s[step]
+            slots_s[step] = jnp.where(sum_rows, got + mine, jnp.maximum(got, mine))
+
+        @pl.when(step < n - 1)
+        def _():
+            small_message(step).start()
+
+        @pl.when(step == n - 1)
+        def _():
+            small_o[...] = slots_s[step]
+
+    def down_lane(d, step):
+        slot = lax.rem(step, 2)
+
+        def own():
+            part = dot_tn(aq_v[d, slot], ddn_v[:, d * half : (d + 1) * half])
+            return part
+
+        def finish(total):
+            gd_o[:, d * half : (d + 1) * half] = total
+
+        aq_copy(d, step, slot).wait()
+
+        @pl.when(step < n - 1)
+        def _():
+            aq_copy(d, step + 1, 1 - slot).start()
+
+        lane(slots_d, send_d, recv_d, d, step, own, finish)
+
+    def rows_of(own_ref, d, step):
+        at = pl.ds(pl.multiple_of(chunk(d, step) * shard, 16), shard)
+        span = own_ref.shape[1] // 2
+        return own_ref[at, d * span : (d + 1) * span].astype(F32)
+
+    def up_lane(d, step):
+        def finish(total):
+            gu_o[:, d * (ff // 2) : (d + 1) * (ff // 2)] = total
+
+        lane(slots_u, send_u, recv_u, d, step, lambda: rows_of(own_u, d, step), finish)
+
+    def qkvo_lane(d, step):
+        def finish(total):
+            if d == 0:
+                gq_o[:, 0 : 2 * width] = total
+            else:
+                gq_o[:, 2 * width : 3 * width] = total[:, 0:width]
+                go_o[...] = total[:, width : 2 * width]
+
+        lane(slots_q, send_q, recv_q, d, step, lambda: rows_of(own_q, d, step), finish)
+
+    def turn(t, _):
+        @pl.when(t < n)
+        def _():
+            for d in range(2):
+                down_lane(d, t)
+            small_step(t)
+
+        @pl.when(jnp.logical_and(t >= 2, t < n + 2))
+        def _():
+            for d in range(2):
+                up_lane(d, t - 2)
+
+        @pl.when(t >= 4)
+        def _():
+            for d in range(2):
+                qkvo_lane(d, t - 4)
+
+        for turn_at in range(4):
+            @pl.when(t == turn_at)
+            def _():
+                for b in range(2 * turn_at, 2 * turn_at + 2):
+                    product(b)
+
+        return 0
+
+    lax.fori_loop(0, n + 4, turn, 0)
+
+    def drain(at, _):
+        for d in range(2):
+            lane(slots_d, send_d, recv_d, d, 0, None, None)(at).wait_send()
+            lane(slots_u, send_u, recv_u, d, 0, None, None)(at).wait_send()
+            lane(slots_q, send_q, recv_q, d, 0, None, None)(at).wait_send()
+        small_message(at).wait_send()
+        return 0
+
+    lax.fori_loop(0, n - 1, drain, 0)
+
+    @pl.when(first)
+    def _():
+        for i in range(row_count):
+            for p in range(1, count):
+                tok_part(i, p).wait_send()
+            tok_own(i).wait()
+
+    @pl.when(jnp.logical_not(first))
+    def _():
+        for i in range(row_count):
+            tok_part(i, 1).wait_recv()
+
+
+def run_grads(count, n, kept, dproj, dbr, dup, ddn, g0, small):
+    x, xq, qkv, lse, ctx, cq, n1, rs1, hq, aq, sl, n2, rs2 = kept
+    rows, seq, width = g0.shape
+    ff = aq.shape[2]
+    flat = lambda a: a.reshape(rows * seq, a.shape[2])
+    tok = rows * seq
+    shard, shard_ff = width // n, ff // n
+    ops = [flat(a) for a in (aq, hq, cq, xq, ddn, dbr, dup, dproj)]
+    vmem = pl.BlockSpec(memory_space=pltpu.VMEM)
+    sem = pltpu.SemaphoreType.DMA
+    return pl.pallas_call(
+        lambda *refs: grad_kernel(count, n, *refs),
+        in_specs=[ANYWHERE] * 8 + [vmem, ANYWHERE],
+        out_specs=[vmem] * 5 + [ANYWHERE],
+        out_shape=[
+            jax.ShapeDtypeStruct((shard, 3 * width), F32),
+            jax.ShapeDtypeStruct((shard, width), F32),
+            jax.ShapeDtypeStruct((shard, ff), F32),
+            jax.ShapeDtypeStruct((shard_ff, width), F32),
+            jax.ShapeDtypeStruct((16, 128), F32),
+            jax.ShapeDtypeStruct((rows, seq // count, width), BF16),
+        ],
+        scratch_shapes=[
+            pltpu.VMEM((2, n, shard_ff, width // 2), BF16),
+            pltpu.VMEM((2, n, shard, ff // 2), BF16),
+            pltpu.VMEM((2, n, shard, 2 * width), BF16),
+            pltpu.VMEM((n, 16, 128), F32),
+            pltpu.VMEM((2, 2, tok, shard_ff), BF16),
+            pltpu.VMEM((tok, width), BF16),
+            pltpu.VMEM((2, tok, width), BF16),
+            pltpu.VMEM((2, tok, width), BF16),
+            pltpu.VMEM((width, ff), BF16),
+            pltpu.VMEM((width, 4 * width), BF16),
+            sem((2, 2)), sem((1,)), sem((3,)), sem((8,)),
+            sem((2, n)), sem((2, n)), sem((2, n)), sem((2, n)), sem((2, n)), sem((2, n)),
+            sem((n,)), sem((n,)), sem((rows, count)), sem((rows,)),
+        ],
+        compiler_params=pltpu.CompilerParams(
+            collective_id=2, has_side_effects=True, vmem_limit_bytes=VMEM_LIMIT,
+        ),
+        cost_estimate=pl.CostEstimate(
+            flops=2 * tok * (4 * width * width + 2 * width * ff), bytes_accessed=tok * 25000, transcendentals=0,
+        ),
+    )(*ops, small, g0)
+
+
 def weight_grad(left, right):
     g = jnp.einsum("rsd,rse->de", left, right, preferred_element_type=F32).astype(BF16)
     return lax.psum_scatter(g, "dp", scatter_dimension=0, tiled=True).astype(F32)
 
 
-def max_over(v, axis):
-    size = lax.axis_size(axis)
-    shift = 1
-    while shift < size:
-        v = jnp.maximum(v, lax.ppermute(v, axis, [(i, (i + shift) % size) for i in range(size)]))
-        shift *= 2
-    return v
+def share_pieces(whole_rows, count, stage):
+    piece = whole_rows.shape[1] // count
+    mine = whole_rows[:, :piece]
+    for p in range(1, count):
+        got = lax.ppermute(whole_rows[:, p * piece : (p + 1) * piece], "pipe", [(0, p)])
+        mine = jnp.where(stage == p, got, mine)
+    return mine
 
 
 def shards(
@@ -759,6 +1063,7 @@
     ln_gain, ln_bias, cotangent,
 ):
     count = lax.axis_size("pipe")
+    n = lax.axis_size("dp")
     width = tokens.shape[2]
     ff = w_up.shape[2]
     b_qkv = jnp.concatenate([bias_qv[:, :width], jnp.zeros_like(bias_qv[:, :width]), bias_qv[:, width:]], 1)
@@ -767,26 +1072,34 @@
     )
     *kept, mixed, peaks = run_forward(count, tokens, lengths, ema_scales, weights)
     x, xq, qkv, lse, ctx, cq, n1, rs1, hq, aq, sl, n2, rs2 = kept
-    dproj, dbr, dup, ddn, grad_tokens, small = run_backward(
+    dproj, dbr, dup, ddn, g0, small = run_backward(
         count, cotangent, lengths, ema_scales, weights, kept
     )
-    batch_max = max_over(jnp.max(peaks, (1, 2))[None], "dp")
-    g_down = weight_grad(aq, ddn)
-    g_up = weight_grad(hq, dup)
-    g_out = weight_grad(cq, dbr)
-    g_qkv = weight_grad(xq, dproj)
-    n = lax.axis_size("dp")
     sums = jnp.sum(small, 0)
     parts, at = [], 0
-    for size in (width, width, width, width, width, width, ff, 3 * width):
+    for size in (width, width, width, width, width, width, ff, width, width, width):
         parts.append(sums[at : at + size])
         at += size
-    gain0, gain1, shift0, shift1, s_out, s_down, s_up, s_qkv = parts
-    s_qv = jnp.concatenate([s_qkv[:width], s_qkv[2 * width :]])
-    packed = jnp.concatenate(
-        [v.reshape(n, -1) for v in (gain0, gain1, shift0, shift1, s_out, s_down, s_up, s_qv)], 1
-    )
-    mine = lax.psum_scatter(packed, "dp", scatter_dimension=0, tiled=True)
+    parts[7:] = [jnp.concatenate([parts[7], parts[9]])]
+    packed = jnp.concatenate([v.reshape(n, -1) for v in parts], 1)
+    peak = jnp.max(peaks, (1, 2))
+    sums_width = packed.shape[1]
+    if n >= 4 and n % 2 == 0 and width // n % 16 == 0 and ff // n % 128 == 0 and sums_width == 9 * 128:
+        top = jnp.broadcast_to(jnp.pad(peak, (0, 124))[None, None], (n, 7, 128))
+        with_peak = jnp.concatenate([packed.reshape(n, 9, 128), top], 1)
+        g_qkv, g_out, g_up, g_down, small_sum, grad_tokens = run_grads(
+            count, n, kept, dproj, dbr, dup, ddn, g0, with_peak
+        )
+        mine = small_sum[:9].reshape(1, sums_width)
+        batch_max = small_sum[9:10, :4]
+    else:
+        g_down = weight_grad(aq, ddn)
+        g_up = weight_grad(hq, dup)
+        g_out = weight_grad(cq, dbr)
+        g_qkv = weight_grad(xq, dproj)
+        mine = lax.psum_scatter(packed, "dp", scatter_dimension=0, tiled=True)
+        batch_max = lax.pmax(peak, "dp")[None]
+        grad_tokens = share_pieces(g0, count, lax.axis_index("pipe"))
     outs, at = [], 0
     for size in (width, width, width, width, width, width, ff, 2 * width):
         outs.append(mine[:, at : at + size // n])

time: 780 us -> 570 us (0.73)
  waiting for transfers between devices: 247 us -> 0 us
  Pallas kernels: 399 us -> 550 us
  matrix products: 48.3 us -> 0 us
  blocking collectives: 37 us -> 0 us
  between operations: 14.3 us -> 0.95 us
    reduce_scatter x4 -> x0, waiting for transfers between devices: 237 us -> none  [weight_grad(): lax.psum_scatter(g, 'dp', scatter_dimension=0, tiled=True).astype(F32)]
    pallas_call x0 -> x1, Pallas kernels: none -> 156 us  [run_grads(): pl.pallas_call(lambda *refs: grad_kernel(count, n, *refs), in_specs=[ANYW...]
    dot_general x4 -> x0, matrix products: 48.3 us -> none  [weight_grad(): jnp.einsum('rsd,rse->de', left, right, preferred_element_type=F32)]
    unnamed x1 -> x0, blocking collectives: 37 us -> none
    ppermute x3 -> x0, waiting for transfers between devices: 9.86 us -> none  [max_over(): lax.ppermute(v, axis, [(i, (i + shift) % size) for i in range(size)])]
    broadcast_in_dim x4 -> x0, other arithmetic: 7.96 us -> none  [the longest x1 2.18 us: shards(): g_up[None]]
  transfers between devices with their start and end apart: 7 -> 0, of which waited for: 5 -> 0; matrix products, arithmetic and copies ran while one was open for 7% -> 0% of each run, Pallas kernels for 0% -> 0%
where the time goes in v2:
time: 570 us; the launch traced here: 566 us
  Pallas kernels  550 us (96%)
  local copies, waits for them, and re-layouts  12 us (2%)
    pallas_call x1, Pallas kernels, run_forward(): pl.pallas_call(lambda *refs: fwd_kernel(count, *refs), grid=(rows,), in_s...  207 us
    pallas_call x1, Pallas kernels, run_backward(): pl.pallas_call(lambda *refs: bwd_kernel(count, *refs), grid=(rows,), in_s...  187 us
    pallas_call x1, Pallas kernels, run_grads(): pl.pallas_call(lambda *refs: grad_kernel(count, n, *refs), in_specs=[ANYW...  156 us

profile of v2, /device:TPU:0, one launch (start us, length us, event | category | flops | bytes accessed | tf_op | source)
XLA Modules:
  0.0 566.2 jit_solution(14982164152739123220)
XLA Ops:
  0.6 0.7 fusion.2
  1.4 0.6 fusion.refs_4_
  2.0 207.0 %shard_map.237 = (bf16[4,512,768]{2,1,0:T(8,128)(2,1)}, bf16[4,512,768]{2,1,0:T(8,128)(2,1)}, bf16[4,512,2304]{2,1,0:T(8,128)(2,1)}, f32[4,512,768]{2,1,0:T(8,12...) custom-call(s32[4]{0:T(128)} %refs_0_.3, ...), custom_call_target="tpu_custom_call" | custom-call | flops 32212254720 | bytes 57344000 | tf_op jit(solution)/shard_map/pallas_call | solution.py:653
  209.0 0.0 copy-start.5
  209.0 187.3 %shard_map.238 = (bf16[4,512,2304]{2,1,0:T(8,128)(2,1)}, bf16[4,512,768]{2,1,0:T(8,128)(2,1)}, bf16[4,512,3072]{2,1,0:T(8,128)(2,1)}, bf16[4,512,768]{2,1,0:T(8,...) custom-call(s32[4]{0:T(128)} %refs_0_.3, f32[1,4]{1,0:T(1,128)} %refs_1_.3, bf16[4,512,768]{2,1,0:T(8,128)(2,1)} %refs_2_.3, ...), custom_call_target="tpu_custom_call" | custom-call | flops 37044092928 | bytes 57344000 | tf_op jit(solution)/shard_map/pallas_call | solution.py:698
  396.3 1.1 reduce_sum.9
  397.4 0.1 concatenate.18
  397.5 0.1 concatenate.19
  397.6 0.1 reshape.157
  397.7 0.1 reshape.158
  397.7 0.1 reshape.159
  397.8 0.1 reshape.160
  397.9 0.1 reshape.161
  397.9 0.1 reshape.162
  398.0 0.1 concatenate.21
  398.1 0.0 copy-done.5
  398.1 0.1 reduce_max.9
  398.3 0.6 pad_maximum_fusion.refs_8_
  398.9 0.0 copy-start.3
  398.9 155.9 %shard_map.239 = (f32[96,2304]{1,0:T(8,128)}, f32[96,768]{1,0:T(8,128)}, f32[96,3072]{1,0:T(8,128)}, f32[384,768]{1,0:T(8,128)}, f32[16,128]{1,0:T(8,128)}, /*index=5*/bf16[4,128,768]{2,1,0:T(8,128)(2,1)}) custom-call(bf16[2048,3072]{1,0:T(8,128)(2,1)} %bitcast.53, bf16[2048,768]{1,0:T(8,128)(2,1)} %bitcast.58, bf16[2048,768]{1,0:T(8,128)(2,1)} %bitcast.57, ...), custom_call_target="tpu_custom_call" | custom-call | flops 28991029248 | bytes 51200000 | tf_op jit(solution)/shard_map/pallas_call | solution.py:1011
  554.8 0.0 copy-start.2
  554.9 0.0 copy-start.4
  554.9 0.0 copy-start.1
  554.9 0.8 slice_bitcast_fusion
  555.7 0.6 slice_bitcast_fusion.2
  556.3 0.6 pad_maximum_fusion.2
  556.9 0.6 slice.168
  557.5 0.6 slice.166
  558.2 1.2 slice.156
  559.4 0.0 copy-done.3
  559.4 0.9 copy.37
  560.2 0.0 copy-start
  560.2 2.2 copy.38
  562.4 0.0 copy-done.2
  562.4 0.9 copy.39
  563.3 0.0 copy-done.4
  563.3 0.7 copy.40
  564.0 0.0 copy-done.1
  564.0 1.0 copy.41
  565.0 0.0 copy-done
  565.0 1.0 copy.42
  (10 shorter events, 0.1 us)
Async XLA Ops:
  209.0 189.2 %copy-start.5 = (f32[4,8,128]{2,1,0:T(8,128)S(1)}, f32[4,8,128]{2,1,0:T(8,128)}, u32[]{:S(2)}) copy-start(f32[4,8,128]{2,1,0:T(8,128)} %get-tuple-element.59) | copy-start | bytes 49156
  398.9 160.4 %copy-start.3 = (bf16[4,128,768]{2,1,0:T(8,128)(2,1)S(1)}, bf16[4,128,768]{2,1,0:T(8,128)(2,1)}, u32[]{:S(2)}) copy-start(bf16[4,128,768]{2,1,0:T(8,128)(2,1)} %get-tuple-element.98) | copy-start | bytes 2359300
  554.8 7.5 %copy-start.2 = (f32[96,2304]{1,0:T(8,128)S(1)}, f32[96,2304]{1,0:T(8,128)}, u32[]{:S(2)}) copy-start(f32[96,2304]{1,0:T(8,128)} %get-tuple-element.62) | copy-start | bytes 2654212
  554.9 8.5 %copy-start.4 = (f32[96,768]{1,0:T(8,128)S(1)}, f32[96,768]{1,0:T(8,128)}, u32[]{:S(2)}) copy-start(f32[96,768]{1,0:T(8,128)} %get-tuple-element.64) | copy-start | bytes 884740
  554.9 9.2 %copy-start.1 = (f32[96,3072]{1,0:T(8,128)S(1)}, f32[96,3072]{1,0:T(8,128)}, u32[]{:S(2)}) copy-start(f32[96,3072]{1,0:T(8,128)} %get-tuple-element.65) | copy-start | bytes 3538948
  560.2 4.8 copy-start
